TPU v7x, 32 devices: a whole 2x2x4 slice. The times are simulated.
32 devices in a mesh: shard: 8 (over z, core), replica: 4 (over y, x).
Axes of the slice: x: 2, y: 2, z: 4, core: 2. Of those that a mesh axis runs over, the one named last changes fastest.
Arguments:
- activations: bfloat16 [2, 2048, 8192], P(None, ('shard', 'replica')), may hold values from -6 to 6
- residual: bfloat16 [2, 2048, 4096], P(None, ('shard', 'replica')), may hold values from -6 to 6
- down_weight: bfloat16 [8192, 4096], P('shard'), may hold values from -0.0625 to 0.0625
- norm_gain: float32 [4096], replicated, may hold values from 0.5 to 1.5
- hard_owner: int32 [2048, 7], P(('shard', 'replica')), may hold values from 0 to 31, all different within a row; in each aligned block of 64 rows (0 to 63, 64 to 127, ...) at most 15 rows name the same one
- hard_row: int32 [2048, 7], P(('shard', 'replica')), may hold values from 0 to 63
Outputs:
- mean_loss: float32 [], replicated
- weight_grad: float32 [8192, 4096], P('shard')
- gain_grad: float32 [4096], replicated
Inputs may be any that keep to these rules, and one draw needn't show every extreme that they name: `hard_owner`: the 7 owners of one query are distinct. Among the 64 queries of one device no device is named more than 15 times, and this bound is met on some devices.
All inputs are finite; a program needn't handle non-finite values.
Results may differ from a plain program's by a relative error of at most 0.025.
Values may be sent and summed in bfloat16 or wider, within the bound.
A program may use at most 128 MiB of HBM per device.

v0:
```python
import jax
import jax.numpy as jnp
from jax import lax
from jax.sharding import PartitionSpec as P

HARD = 7


epsilon = 1e-05
sharpness_divisor = 0.02


def normalize_rows(stream, norm_gain):
    inv_rms = lax.rsqrt(jnp.mean(stream * stream, axis=-1, keepdims=True) + epsilon)
    normed = stream * inv_rms
    scaled = normed * norm_gain
    length = jnp.sqrt(jnp.sum(scaled * scaled, axis=-1, keepdims=True))
    return (inv_rms, normed, length, scaled / length)


def backward_rows(normalized_entry_sensitivity, inv_rms, normed, length, unit_f32, norm_gain):
    grad_scaled = (
        normalized_entry_sensitivity
        - unit_f32 * jnp.sum(unit_f32 * normalized_entry_sensitivity, axis=-1, keepdims=True)
    ) / length
    gain_terms = jnp.sum(grad_scaled * normed, axis=0)
    grad_normed = grad_scaled * norm_gain
    grad_stream = inv_rms * (
        grad_normed - normed * jnp.mean(grad_normed * normed, axis=-1, keepdims=True)
    )
    return (gain_terms, grad_stream.astype(jnp.bfloat16))


def softmax_terms(shared_pool_affinity, mined_distractor_affinity):
    width = shared_pool_affinity.shape[-1]
    cosine_affinity_matrix = (
        jnp.concatenate([shared_pool_affinity, mined_distractor_affinity], axis=-1)
        / sharpness_divisor
    )
    expo = jnp.exp(cosine_affinity_matrix)
    totals = jnp.sum(expo, axis=-1, keepdims=True)
    matching_target_index = jnp.diagonal(shared_pool_affinity) / sharpness_divisor
    losses = jnp.log(totals[:, 0]) - matching_target_index
    identity = jnp.eye(width, dtype=jnp.float32)
    target = jnp.concatenate([identity, jnp.zeros_like(mined_distractor_affinity)], axis=-1)
    weights = (expo / totals - target).astype(jnp.bfloat16)
    return (jnp.sum(losses), weights[:, :width], weights[:, width:])


def per_device(activations, residual, down_weight, norm_gain, hard_owner, hard_row):
    query_count = activations.shape[1]
    width = down_weight.shape[1]
    rows = activations.reshape(2 * query_count, activations.shape[2])
    spread_rows = lax.all_to_all(rows, "shard", split_axis=1, concat_axis=0, tiled=True)
    picked = spread_rows
    mixed = lax.psum_scatter(
        jnp.dot(picked, down_weight, preferred_element_type=jnp.float32).astype(jnp.bfloat16),
        "shard",
        scatter_dimension=0,
        tiled=True,
    ).astype(jnp.float32)
    stream = residual.reshape(2 * query_count, width).astype(jnp.float32) + mixed
    inv_rms, normed, length, unit_f32 = normalize_rows(stream, norm_gain)
    unit = unit_f32.astype(jnp.bfloat16)
    query_emb = unit[:query_count]
    passage_emb = unit[query_count:]
    shared_pool_affinity = jnp.dot(query_emb, passage_emb.T, preferred_element_type=jnp.float32)
    devices = lax.axis_size(("shard", "replica"))
    capacity = max(2, query_count * HARD // devices + 1)
    flat_owner = hard_owner.reshape(-1)
    owner_hits = (flat_owner[:, None] == jnp.arange(devices, dtype=jnp.int32)[None, :]).astype(
        jnp.int32
    )
    earlier = jnp.cumsum(owner_hits, axis=0) - owner_hits
    position = jnp.sum(earlier * owner_hits, axis=1)
    slot_index = flat_owner * capacity + position
    wanted = jnp.full((devices * capacity,), -1, jnp.int32).at[slot_index].set(hard_row.reshape(-1))
    incoming = lax.all_to_all(
        wanted.reshape(devices, capacity),
        ("shard", "replica"),
        split_axis=0,
        concat_axis=0,
        tiled=True,
    )
    incoming_flat = incoming.reshape(-1)
    valid_slots = incoming_flat >= 0
    safe_rows = jnp.maximum(incoming_flat, 0)
    served = passage_emb[safe_rows]
    returned = lax.all_to_all(
        served.reshape(devices, capacity, width),
        ("shard", "replica"),
        split_axis=0,
        concat_axis=0,
        tiled=True,
    )
    hard_emb = returned.reshape(devices * capacity, width)[slot_index].reshape(
        query_count, HARD, width
    )
    mined_distractor_affinity = jnp.einsum(
        "qd,qkd->qk", query_emb, hard_emb, preferred_element_type=jnp.float32
    )
    loss_part, grad_local, grad_hard = softmax_terms(
        shared_pool_affinity, mined_distractor_affinity
    )
    request_sensitivity = jnp.dot(grad_local, passage_emb, preferred_element_type=jnp.float32)
    document_sensitivity = jnp.dot(grad_local.T, query_emb, preferred_element_type=jnp.float32)
    request_sensitivity = request_sensitivity + jnp.einsum(
        "qk,qkd->qd", grad_hard, hard_emb, preferred_element_type=jnp.float32
    )
    pair_terms = (
        grad_hard.astype(jnp.float32)[:, :, None] * query_emb.astype(jnp.float32)[:, None, :]
    )
    outgoing_terms = (
        jnp.zeros((devices * capacity, width), jnp.float32)
        .at[slot_index]
        .set(pair_terms.reshape(query_count * HARD, width))
    )
    arrived = lax.all_to_all(
        outgoing_terms.reshape(devices, capacity, width).astype(jnp.bfloat16),
        ("shard", "replica"),
        split_axis=0,
        concat_axis=0,
        tiled=True,
    ).astype(jnp.float32)
    arrived = arrived.reshape(devices * capacity, width) * valid_slots.astype(jnp.float32)[:, None]
    document_sensitivity = document_sensitivity.at[safe_rows].add(arrived)
    normalized_entry_sensitivity = (
        jnp.concatenate([request_sensitivity, document_sensitivity], axis=0) / sharpness_divisor
    )
    gain_part, grad_stream = backward_rows(
        normalized_entry_sensitivity, inv_rms, normed, length, unit_f32, norm_gain
    )
    picked = spread_rows
    local_grad = lax.dot_general(
        picked,
        lax.all_gather(grad_stream, "shard", axis=0, tiled=True),
        (((0,), (0,)), ((), ())),
        preferred_element_type=jnp.float32,
    )
    weight_grad = lax.psum(local_grad.astype(jnp.bfloat16), "replica").astype(jnp.float32)
    gain_grad, loss_total = lax.psum((gain_part, loss_part), ("shard", "replica"))
    mean_loss = loss_total / (query_count * devices)
    return (mean_loss, weight_grad, gain_grad)


def solution(mesh):
    in_specs = (
        P(None, ("shard", "replica"), None),
        P(None, ("shard", "replica"), None),
        P("shard", None),
        P(),
        P(("shard", "replica"), None),
        P(("shard", "replica"), None),
    )
    out_specs = (P(), P("shard", None), P())
    return jax.shard_map(
        per_device, mesh=mesh, in_specs=in_specs, out_specs=out_specs, check_vma=False
    )
```

profile of v0, /device:TPU:0, one launch (start us, length us, event | category | flops | bytes accessed | tf_op | source)
XLA Modules:
  0.0 748.5 jit_solution(15933643579077244676)
XLA Ops:
  7.2 3.0 copy.37
  10.2 1.2 copy.23
  11.4 55.5 %all_to_all.38 = bf16[128,8,1024]{2,0,1:T(8,128)(2,1)S(1)} all-to-all(bf16[128,8,1024]{2,0,1:T(8,128)(2,1)S(1)} %copy.23), channel_id=1, replica_groups=mesh['shard'=8,'replica'=4] {'shard'}, dimensions={1} | all-to-all | bytes 4194304 | tf_op jit(solution)/shard_map/all_to_all | solution.py:54
  66.8 1.3 copy-done.7
  68.1 10.8 %convolution_convert_fusion = bf16[1024,4096]{1,0:T(8,128)(2,1)} fusion(bf16[1024,1024]{1,0:T(8,128)(2,1)S(1)} %bitcast.58, bf16[1024,4096]{1,0:T(8,128)(2,1)S(1)} %copy-done.11), kind=kOutput, calls=%fused_computation.9 | convolution fusion | flops 8594128896 | bytes 18874368 | tf_op jit(solution)/shard_map/dot_general | solution.py:57
  79.0 0.7 copy-done.9
  80.4 1.2 reduce-window.6
  81.6 0.2 slice_reduce_fusion
  82.0 2.9 scatter_custom_fusion
  85.0 10.7 %all_to_all.39 = s32[32,1,15]{2,1,0:T(1,128)S(1)} all-to-all(s32[32,1,15]{2,1,0:T(1,128)S(1)} %bitcast.62), channel_id=1, replica_groups=mesh['shard'=8,'replica'=4] {'shard','replica'}, dimensions={0} | all-to-all | bytes 3840 | tf_op jit(solution)/shard_map/all_to_all | solution.py:78
  95.8 72.1 %reduce-scatter.2.cloned.1.call-done = bf16[128,4096]{1,0:T(8,128)(2,1)} async-done(((bf16[1024,4096]{1,0:T(8,128)(2,1)}), bf16[128,4096]{1,0:T(8,128)(2,1)}) %reduce-scatter.2.cloned.1.call-update) | async-done | bytes 1048592 | tf_op jit(solution)/shard_map/reduce_scatter | solution.py:56
  167.9 1.7 multiply_reduce_fusion.4
  169.7 0.6 multiply_reduce_fusion.3
  170.3 0.5 fusion.27
  170.8 1.0 copy-done.2
  171.9 1.3 slice_convert_fusion
  173.2 4.3 gather_fusion
  177.5 5.1 reshape.133
  182.6 4.0 all-to-all-start.2
  186.6 4.4 mul.119
  191.0 7.0 mul.120
  198.1 0.3 fusion.12
  198.4 82.7 %all-to-all-done.2 = bf16[32,15,4096]{2,1,0:T(8,128)(2,1)} async-done(((bf16[32,15,4096]{2,1,0:T(8,128)(2,1)}), bf16[32,15,4096]{2,1,0:T(8,128)(2,1)}, u32[]{:S(2)}, u32[]{:S(2)}) %all-to-all-start.2) | async-done | bytes 3932192 | tf_op jit(solution)/shard_map/all_to_all | solution.py:89
  281.1 5.1 reshape.134
  286.2 11.0 %gather_fusion.1 = bf16[448,4096]{1,0:T(8,128)(2,1)} fusion(bf16[480,4096]{1,0:T(8,128)(2,1)} %reshape.134, s32[1024]{0:T(1024)S(1)} %pad_clamp_fusion), kind=kCustom, calls=%fused_computation.1 | custom fusion | bytes 7341824 | tf_op jit(solution)/shard_map/gather | solution.py:96
  297.2 5.1 reshape.135
  302.3 5.1 fusion.8
  307.4 0.2 fusion.22
  307.9 11.8 %scatter_custom_fusion.1 = f32[480,4096]{1,0:T(8,128)} fusion(s32[448]{0:T(512)S(1)} %bitcast.65, f32[448,4096]{1,0:T(8,128)} %mul.120, f32[]{:T(128)} %constant.15.clone.1, f32[448]{0:T(512)S(1)} %reshape.140), kind=kCustom, calls=%fused_computation.10 | custom fusion | flops 1835008 | bytes 15206404 | tf_op jit(solution)/shard_map/scatter | solution.py:116
  319.8 5.7 convert_element_type.64
  325.5 5.1 convert_element_type.65
  330.6 5.5 all-to-all-start.3
  336.4 1.3 fusion.10
  337.7 3.4 fusion.17
  341.1 1.8 convolution_add_fusion
  342.9 87.6 %all-to-all-done.3 = bf16[32,15,4096]{2,1,0:T(8,128)(2,1)} async-done(((bf16[32,15,4096]{2,1,0:T(8,128)(2,1)}), bf16[32,15,4096]{2,1,0:T(8,128)(2,1)}, u32[]{:S(2)}, u32[]{:S(2)}) %all-to-all-start.3) | async-done | bytes 3932192 | tf_op jit(solution)/shard_map/all_to_all | solution.py:118
  430.5 6.2 reshape.142
  436.7 16.1 %scatter_custom_fusion.2 = f32[64,4096]{1,0:T(8,128)} fusion(f32[64,4096]{1,0:T(8,128)} %fusion.10, s32[480]{0:T(512)S(1)} %reshape.146, f32[480,4096]{1,0:T(8,128)} %reshape.142, f32[480]{0:T(512)S(1)} %reshape.143), kind=kCustom, calls=%fused_computation.7 | custom fusion | flops 3932160 | bytes 8914944 | tf_op jit(solution)/shard_map/scatter-add | solution.py:126
  452.9 2.0 multiply_reduce_fusion.2
  454.9 1.4 multiply_reduce_fusion
  456.3 1.7 multiply_convert_fusion
  458.1 83.3 %all-gather.2.cloned.1.call-done = bf16[1024,4096]{1,0:T(8,128)(2,1)} async-done(((bf16[128,4096]{1,0:T(8,128)(2,1)}), bf16[1024,4096]{1,0:T(8,128)(2,1)}) %all-gather.2.cloned.1.call-update) | async-done | bytes 8388624 | tf_op jit(solution)/shard_map/all_gather | solution.py:136
  541.3 14.9 %convert_bitcast_fusion = bf16[1024,4096]{0,1:T(8,128)(2,1)} fusion(bf16[1024,4096]{1,0:T(8,128)(2,1)} %all-gather.2.cloned.1.call-done, bf16[1024,1024]{1,0:T(8,128)(2,1)} %bitcast.59), kind=kOutput, calls=%fused_computation.6 | convolution fusion | flops 8594128896 | bytes 18874368 | tf_op jit(solution)/shard_map/dot_general | solution.py:134
  556.3 0.8 gather_fusion.2
  557.1 0.6 subtract_reduce_fusion
  557.7 39.6 %all-reduce.2 = (f32[]{:T(128)}, f32[4096]{0:T(1024)}) all-reduce(f32[]{:T(128)} %subtract_reduce_fusion, f32[4096]{0:T(1024)S(1)} %get-tuple-element.15), channel_id=1, replica_groups=mesh['shard'=8,'replica'=4] {'shard','replica'}, use_global_device_ids=true, to_apply=%region_9.10 | all-reduce | flops 4097 | bytes 32776 | tf_op jit(solution)/shard_map/psum | solution.py:141
  597.9 130.3 %all-reduce.5.cloned.1.call-done = bf16[1024,4096]{0,1:T(8,128)(2,1)} async-done(((bf16[1024,4096]{0,1:T(8,128)(2,1)}), bf16[1024,4096]{0,1:T(8,128)(2,1)}) %all-reduce.5.cloned.1.call-update) | async-done | bytes 8388624 | tf_op jit(solution)/shard_map/psum | solution.py:140
  728.3 12.3 %copy.30 = f32[1024,4096]{1,0:T(8,128)} copy(bf16[1024,4096]{0,1:T(8,128)(2,1)} %all-reduce.5.cloned.1.call-done) | data formatting | bytes 25165824
  (56 shorter events, 1.9 us)
Async XLA Ops:
  7.2 160.8 %reduce-scatter.2.cloned.1.call-start = ((), (), s32[]{:S(2)}) async-start(), calls=%async_computation.5 | async-start | bytes 9437184 | tf_op jit(solution)/shard_map/reduce_scatter | solution.py:56
  10.2 57.9 %copy-start.11 = (bf16[1024,4096]{1,0:T(8,128)(2,1)S(1)}, bf16[1024,4096]{1,0:T(8,128)(2,1)}, u32[]{:S(2)}) copy-start(bf16[1024,4096]{1,0:T(8,128)(2,1)} %param.8) | copy-start | bytes 25165828
  66.8 1.3 copy-start.7
  78.9 0.7 copy-start.9
  79.0 1.0 copy-start.10
  79.0 89.0 %copy-start = (bf16[2,64,4096]{2,1,0:T(8,128)(2,1)S(1)}, bf16[2,64,4096]{2,1,0:T(8,128)(2,1)}, u32[]{:S(2)}) copy-start(bf16[2,64,4096]{2,1,0:T(8,128)(2,1)} %param.7) | copy-start | bytes 3145732
  79.6 90.0 %copy-start.8 = (f32[4096]{0:T(1024)S(1)}, f32[4096]{0:T(1024)}, u32[]{:S(2)}) copy-start(f32[4096]{0:T(1024)} %param.9) | copy-start | bytes 49156
  167.9 1.8 copy-start.1
  170.8 1.0 copy-start.2
  182.6 4.0 copy-start.6
  182.6 98.5 %all-to-all-start.2 = ((bf16[32,15,4096]{2,1,0:T(8,128)(2,1)}), bf16[32,15,4096]{2,1,0:T(8,128)(2,1)}, u32[]{:S(2)}, u32[]{:S(2)}) async-start(bf16[32,15,4096]{2,1,0:T(8,128)(2,1)} %reshape.133), calls=%async_computation.3 | async-start | bytes 8388608 | tf_op jit(solution)/shard_map/all_to_all | solution.py:89
  191.0 7.0 copy-start.3
  330.6 99.9 %all-to-all-start.3 = ((bf16[32,15,4096]{2,1,0:T(8,128)(2,1)}), bf16[32,15,4096]{2,1,0:T(8,128)(2,1)}, u32[]{:S(2)}, u32[]{:S(2)}) async-start(bf16[32,15,4096]{2,1,0:T(8,128)(2,1)} %convert_element_type.65), calls=%async_computation.4 | async-start | bytes 8388608 | tf_op jit(solution)/shard_map/all_to_all | solution.py:118
  336.2 205.2 %all-gather.2.cloned.1.call-start = ((), (), s32[]{:S(2)}) async-start(), calls=%async_computation.6 | async-start | bytes 9437184 | tf_op jit(solution)/shard_map/all_gather | solution.py:136
  436.7 16.2 %copy-start.4 = (f32[64,4096]{1,0:T(8,128)S(1)}, f32[64,4096]{1,0:T(8,128)}, u32[]{:S(2)}) copy-start(f32[64,4096]{1,0:T(8,128)} %convolution_add_fusion) | copy-start | bytes 3145732
  452.8 2.1 copy-start.5
  458.0 270.2 %all-reduce.5.cloned.1.call-start = ((), (), s32[]{:S(2)}) async-start(), calls=%async_computation.7 | async-start | bytes 16777216 | tf_op jit(solution)/shard_map/psum | solution.py:140
Sparse Core Ops, SparseCore 0:
  79.1 88.7 reduce-scatter.1
  458.1 83.1 all-gather.1
  556.4 171.8 all-reduce.4
where the time goes:
time: 758 us; the launch traced here: 748 us
  waiting for transfers between devices  456 us (60%)
  blocking collectives  106 us (14%)
  local copies, waits for them, and re-layouts  78 us (10%)
  other arithmetic  45.5 us (6%)
  matrix products  37.6 us (5%)
  between operations  16 us (2%)
  starting transfers between devices  9.62 us (1%)
    psum x1, waiting for transfers between devices, per_device(): lax.psum(local_grad.astype(jnp.bfloat16), 'replica').astype(jnp.float32)  130 us
    all_to_all x1, waiting for transfers between devices, per_device(): lax.all_to_all(outgoing_terms.reshape(devices, capacity, width).astype(jn...  87.6 us
    all_gather x1, waiting for transfers between devices, per_device(): lax.all_gather(grad_stream, 'shard', axis=0, tiled=True)  83.3 us
    all_to_all x1, waiting for transfers between devices, per_device(): lax.all_to_all(served.reshape(devices, capacity, width), ('shard', 'repli...  82.7 us
    reduce_scatter x1, waiting for transfers between devices, per_device(): lax.psum_scatter(jnp.dot(picked, down_weight, preferred_element_type=jnp....  72.1 us
    all_to_all x1, blocking collectives, per_device(): lax.all_to_all(rows, 'shard', split_axis=1, concat_axis=0, tiled=True)  55.5 us
    psum x1, blocking collectives, per_device(): lax.psum((gain_part, loss_part), ('shard', 'replica'))  39.6 us
    unnamed x28, local copies, waits for them, and re-layouts  18.6 us
  transfers between devices with their start and end apart: 5, of which 5 were waited for; matrix products, arithmetic and copies ran while one was open for 3% of the time, Pallas kernels for 0%

commit v1 on v0

v1 whole, which is shorter than its diff:
```python
import functools

import jax
import jax.numpy as jnp
from jax import lax
from jax.experimental import pallas as pl
from jax.experimental.pallas import tpu as pltpu
from jax.sharding import PartitionSpec as P

HARD = 7
LANES = 128


epsilon = 1e-05
sharpness_divisor = 0.02


def normalize_rows(stream, norm_gain):
    inv_rms = lax.rsqrt(jnp.mean(stream * stream, axis=-1, keepdims=True) + epsilon)
    normed = stream * inv_rms
    scaled = normed * norm_gain
    length = jnp.sqrt(jnp.sum(scaled * scaled, axis=-1, keepdims=True))
    return (inv_rms, length, scaled / length)


def softmax_terms(local_score, hard_score):
    width = local_score.shape[-1]
    logits = jnp.concatenate([local_score, hard_score], axis=-1) / sharpness_divisor
    expo = jnp.exp(logits)
    totals = jnp.sum(expo, axis=-1, keepdims=True)
    positive = jnp.diagonal(local_score) / sharpness_divisor
    losses = jnp.log(totals[:, 0]) - positive
    identity = jnp.eye(width, dtype=jnp.float32)
    target = jnp.concatenate([identity, jnp.zeros_like(hard_score)], axis=-1)
    weights = (expo / totals - target).astype(jnp.bfloat16).astype(jnp.float32)
    return (losses[:, None], weights, weights * logits)


def pick_kernel(q_ref, p_ref, name_ref, out_ref):
    score = lax.dot_general(
        q_ref[...], p_ref[...], (((1,), (1,)), ((), ())), preferred_element_type=jnp.float32
    )
    name = name_ref[...]
    lane, group = name % LANES, name // LANES
    found = jnp.zeros(out_ref.shape, jnp.float32)
    for block in range(p_ref.shape[0] // LANES):
        here = jnp.take_along_axis(score[:, block * LANES : (block + 1) * LANES], lane, axis=1)
        found = jnp.where(group == block, here, found)
    out_ref[...] = found


def pick_scores(queries, passages, names, block):
    total, feats = queries.shape
    return pl.pallas_call(
        pick_kernel,
        grid=(total // block,),
        in_specs=[
            pl.BlockSpec((block, feats), lambda i: (i, 0)),
            pl.BlockSpec((total, feats), lambda i: (0, 0)),
            pl.BlockSpec((block, LANES), lambda i: (i, 0)),
        ],
        out_specs=pl.BlockSpec((block, LANES), lambda i: (i, 0)),
        out_shape=jax.ShapeDtypeStruct((total, LANES), jnp.float32),
        compiler_params=pltpu.CompilerParams(vmem_limit_bytes=48 * 1024 * 1024),
    )(queries, passages, names)


def spread_kernel(group_rows, q_ref, p_ref, name_ref, pack_ref, gq_ref, gp_ref, tp_ref):
    step = pl.program_id(0)

    @pl.when(step == 0)
    def _():
        gp_ref[...] = jnp.zeros_like(gp_ref)
        tp_ref[...] = jnp.zeros_like(tp_ref)

    block, total = q_ref.shape[0], p_ref.shape[0]
    column = lax.broadcasted_iota(jnp.int32, (block, total), 1)
    weight = jnp.zeros((block, total), jnp.float32)
    share = jnp.zeros((block, total), jnp.float32)
    for k in range(HARD):
        hit = column == name_ref[:, k : k + 1]
        weight = jnp.where(hit, pack_ref[:, group_rows + k : group_rows + k + 1], weight)
        share = jnp.where(
            hit, pack_ref[:, group_rows + HARD + k : group_rows + HARD + k + 1], share
        )
    tp_ref[...] += jnp.sum(share, axis=0, keepdims=True)
    weight = weight.astype(jnp.bfloat16)
    gq_ref[...] = jnp.dot(weight, p_ref[...], preferred_element_type=jnp.float32)
    gp_ref[...] += lax.dot_general(
        weight, q_ref[...], (((0,), (0,)), ((), ())), preferred_element_type=jnp.float32
    )
    for part in range(block // group_rows):
        mine = slice(part * group_rows, (part + 1) * group_rows)
        there = pl.ds(pl.multiple_of(step * block + part * group_rows, group_rows), group_rows)
        local = pack_ref[mine, :group_rows].astype(jnp.bfloat16)
        gq_ref[mine, :] += jnp.dot(local, p_ref[there, :], preferred_element_type=jnp.float32)
        gp_ref[there, :] += lax.dot_general(
            local, q_ref[mine, :], (((0,), (0,)), ((), ())), preferred_element_type=jnp.float32
        )


def spread_grads(queries, passages, names, pack, block, group_rows):
    total, feats = queries.shape
    return pl.pallas_call(
        functools.partial(spread_kernel, group_rows),
        grid=(total // block,),
        in_specs=[
            pl.BlockSpec((block, feats), lambda i: (i, 0)),
            pl.BlockSpec((total, feats), lambda i: (0, 0)),
            pl.BlockSpec((block, LANES), lambda i: (i, 0)),
            pl.BlockSpec((block, LANES), lambda i: (i, 0)),
        ],
        out_specs=[
            pl.BlockSpec((block, feats), lambda i: (i, 0)),
            pl.BlockSpec((total, feats), lambda i: (0, 0)),
            pl.BlockSpec((1, total), lambda i: (0, 0)),
        ],
        out_shape=[
            jax.ShapeDtypeStruct((total, feats), jnp.float32),
            jax.ShapeDtypeStruct((total, feats), jnp.float32),
            jax.ShapeDtypeStruct((1, total), jnp.float32),
        ],
        compiler_params=pltpu.CompilerParams(vmem_limit_bytes=48 * 1024 * 1024),
    )(queries, passages, names, pack)


def per_device(activations, residual, down_weight, norm_gain, hard_owner, hard_row):
    everywhere = ("shard", "replica")
    n_shard, n_replica = lax.axis_size("shard"), lax.axis_size("replica")
    devices = n_shard * n_replica
    count = activations.shape[1]
    width = down_weight.shape[1]
    hidden = down_weight.shape[0]
    feats = width // devices
    total = count * devices
    block = 256 if total <= 2048 else 64

    name = jnp.pad(hard_owner * count + hard_row, ((0, 0), (0, LANES - HARD)))
    names = lax.all_gather(name, everywhere, axis=0, tiled=True)

    rows = activations.reshape(2 * count, activations.shape[2])
    spread_rows = lax.all_to_all(rows, "shard", split_axis=1, concat_axis=0, tiled=True)
    terms = jnp.dot(spread_rows, down_weight, preferred_element_type=jnp.float32)
    mixed = lax.psum_scatter(
        terms.astype(jnp.bfloat16), "shard", scatter_dimension=0, tiled=True
    ).astype(jnp.float32)
    all_rows = lax.all_gather(spread_rows, "replica", axis=0, tiled=False)
    all_rows = all_rows.reshape(n_replica, n_shard, 2, count, hidden)
    all_rows = all_rows.transpose(2, 1, 0, 3, 4).reshape(2 * total, hidden)

    stream = residual.reshape(2 * count, width).astype(jnp.float32) + mixed
    inv_rms, length, unit_f32 = normalize_rows(stream, norm_gain)
    unit = unit_f32.astype(jnp.bfloat16)
    held = unit.astype(jnp.float32)
    square = jnp.sum(held * held, axis=-1, keepdims=True)

    cut = unit.reshape(2 * count, n_replica, n_shard, feats).transpose(2, 1, 0, 3)
    cut = cut.reshape(devices, 2 * count, feats)
    cut = lax.all_to_all(cut, everywhere, split_axis=0, concat_axis=0, tiled=True)
    queries = cut[:, :count].reshape(total, feats)
    passages = cut[:, count:].reshape(total, feats)

    local_score = jnp.dot(unit[:count], unit[count:].T, preferred_element_type=jnp.float32)
    partial = pick_scores(queries, passages, names, block)[:, :HARD]
    partial = lax.all_to_all(
        partial.reshape(devices, count * HARD), everywhere, split_axis=0, concat_axis=0, tiled=True
    )
    hard_score = jnp.sum(partial, axis=0).reshape(count, HARD)
    losses, weights, shares = softmax_terms(local_score, hard_score)

    pack = jnp.concatenate(
        [
            weights,
            shares[:, count:],
            jnp.sum(shares, axis=1, keepdims=True),
            jnp.sum(shares[:, :count], axis=0)[:, None],
            inv_rms.reshape(2, count).T,
            length.reshape(2, count).T,
            square.reshape(2, count).T,
            losses,
        ],
        axis=1,
    )
    pack = jnp.pad(pack, ((0, 0), (0, LANES - pack.shape[1])))
    pack = lax.all_gather(pack, everywhere, axis=0, tiled=True)
    at = count + 2 * HARD

    def both(first):
        return jnp.stack([pack[:, first], pack[:, first + 1]])[:, :, None]

    grad_q, grad_p, extra = spread_grads(queries, passages, names, pack, block, count)
    dots = both(at) + jnp.stack([jnp.zeros((total,), jnp.float32), extra[0]])[:, :, None]
    inv_rms, length, square = both(at + 2), both(at + 4), both(at + 6)
    mean_loss = jnp.sum(pack[:, at + 8]) / total

    start = lax.axis_index("replica") * (width // n_replica) + lax.axis_index("shard") * feats
    gain = lax.dynamic_slice(norm_gain, (start,), (feats,))
    held = jnp.stack([queries, passages]).astype(jnp.float32)
    grad_unit = jnp.stack([grad_q, grad_p]) / sharpness_divisor
    grad_scaled = (grad_unit - held * dots) / length
    normed = held * length / gain
    gain_part = jnp.sum(grad_scaled * normed, axis=(0, 1))
    mean = (dots - dots * square) / width
    grad_stream = inv_rms * (grad_scaled * gain - normed * mean)
    grad_stream = grad_stream.astype(jnp.bfloat16).reshape(2 * total, feats)

    gain_grad = lax.all_gather(gain_part, everywhere, axis=0, tiled=True)
    gain_grad = gain_grad.reshape(n_shard, n_replica, feats).transpose(1, 0, 2).reshape(width)

    columns = lax.all_gather(grad_stream, "shard", axis=1, tiled=True)
    quarter = lax.dot_general(
        all_rows, columns, (((0,), (0,)), ((), ())), preferred_element_type=jnp.float32
    )
    weight_grad = lax.all_gather(
        quarter.astype(jnp.bfloat16), "replica", axis=1, tiled=True
    ).astype(jnp.float32)
    return (mean_loss, weight_grad, gain_grad)


def solution(mesh):
    in_specs = (
        P(None, ("shard", "replica"), None),
        P(None, ("shard", "replica"), None),
        P("shard", None),
        P(),
        P(("shard", "replica"), None),
        P(("shard", "replica"), None),
    )
    out_specs = (P(), P("shard", None), P())
    return jax.shard_map(
        per_device, mesh=mesh, in_specs=in_specs, out_specs=out_specs, check_vma=False
    )
```

time: 758 us -> 609 us (0.80); the launches traced: 748 us -> 608 us
  waiting for transfers between devices: 456 us -> 345 us
  Pallas kernels: 0 us -> 41.9 us
  local copies, waits for them, and re-layouts: 78 us -> 36.5 us
  other arithmetic: 45.5 us -> 13.3 us
  blocking collectives: 106 us -> 121 us
  matrix products: 37.6 us -> 25.9 us
    all_gather x1 -> x5, waiting for transfers between devices: 83.3 us -> 224 us  [the longest x1 75.4 us: per_device(): columns = lax.all_gather(grad_stream, 'shard', axis=1, tiled=True)]
    all_to_all x2, waiting for transfers between devices: 170 us -> 32 us  [the longest x1 26.2 us: per_device(): lax.all_to_all(cut, everywhere, split_axis=0, concat_axis=0, tiled=True)]
    psum x1 -> x0, waiting for transfers between devices: 130 us -> none  [per_device(): lax.psum(local_grad.astype(jnp.bfloat16), 'replica').astype(jnp.float32)]
    all_gather x0 -> x1, blocking collectives: none -> 65.1 us  [per_device(): gain_grad = lax.all_gather(gain_part, everywhere, axis=0, tiled=True)]
    pallas_call x0 -> x2, Pallas kernels: none -> 41.9 us  [the longest x1 29.7 us: spread_grads(): pl.pallas_call(functools.partial(spread_kernel, group_rows), grid=(total...]
    psum x1 -> x0, blocking collectives: 39.6 us -> none  [per_device(): lax.psum((gain_part, loss_part), ('shard', 'replica'))]
    reshape x5 -> x1, local copies, waits for them, and re-layouts: 21.6 us -> 0.13 us  [per_device(): hard_score = jnp.sum(partial, axis=0).reshape(count, HARD)]
    reduce_scatter x1, waiting for transfers between devices: 72.1 us -> 88.7 us  [per_device(): lax.psum_scatter(terms.astype(jnp.bfloat16), 'shard', scatter_dimension=0...]
  transfers between devices with their start and end apart: 5 -> 8, of which waited for: 5 -> 8; matrix products, arithmetic and copies ran while one was open for 3% -> 4% of each run, Pallas kernels for 0% -> 5%
where the time goes in v1:
time: 609 us; the launch traced here: 608 us
  waiting for transfers between devices  345 us (57%)
  blocking collectives  121 us (20%)
  Pallas kernels  41.9 us (7%)
  local copies, waits for them, and re-layouts  36.5 us (6%)
  matrix products  25.9 us (4%)
  between operations  17.7 us (3%)
  other arithmetic  13.3 us (2%)
  starting transfers between devices  7.15 us (1%)
    reduce_scatter x1, waiting for transfers between devices, per_device(): lax.psum_scatter(terms.astype(jnp.bfloat16), 'shard', scatter_dimension=0...  88.7 us
    all_gather x1, waiting for transfers between devices, per_device(): columns = lax.all_gather(grad_stream, 'shard', axis=1, tiled=True)  75.4 us
    all_gather x1, blocking collectives, per_device(): gain_grad = lax.all_gather(gain_part, everywhere, axis=0, tiled=True)  65.1 us
    all_to_all x1, blocking collectives, per_device(): lax.all_to_all(rows, 'shard', split_axis=1, concat_axis=0, tiled=True)  55.5 us
    all_gather x1, waiting for transfers between devices, per_device(): pack = lax.all_gather(pack, everywhere, axis=0, tiled=True)  49.7 us
    all_gather x1, waiting for transfers between devices, per_device(): all_rows = lax.all_gather(spread_rows, 'replica', axis=0, tiled=False)  47.2 us
    all_gather x1, waiting for transfers between devices, per_device(): names = lax.all_gather(name, everywhere, axis=0, tiled=True)  32.2 us
    pallas_call x1, Pallas kernels, spread_grads(): pl.pallas_call(functools.partial(spread_kernel, group_rows), grid=(total...  29.7 us
  transfers between devices with their start and end apart: 8, of which 8 were waited for; matrix products, arithmetic and copies ran while one was open for 4% of the time, Pallas kernels for 5%

profile of v1, /device:TPU:0, one launch (start us, length us, event | category | flops | bytes accessed | tf_op | source)
XLA Modules:
  0.0 608.3 jit_solution(3387390415747417170)
XLA Ops:
  8.0 3.0 copy.89
  11.1 1.2 copy.76
  12.2 55.5 %all_to_all.34 = bf16[128,8,1024]{2,0,1:T(8,128)(2,1)S(1)} all-to-all(bf16[128,8,1024]{2,0,1:T(8,128)(2,1)S(1)} %copy.76), channel_id=1, replica_groups=mesh['shard'=8,'replica'=4] {'shard'}, dimensions={1} | all-to-all | bytes 4194304 | tf_op jit(solution)/shard_map/all_to_all | solution.py:142
  67.7 1.3 copy-done.5
  69.0 10.8 %convolution_convert_fusion = bf16[1024,4096]{1,0:T(8,128)(2,1)} fusion(bf16[1024,1024]{1,0:T(8,128)(2,1)S(1)} %bitcast.110, bf16[1024,4096]{1,0:T(8,128)(2,1)S(1)} %copy-done.9), kind=kOutput, calls=%fused_computation.1 | convolution fusion | flops 8594128896 | bytes 18874368 | tf_op jit(solution)/shard_map/dot_general | solution.py:143
  79.9 88.7 %reduce-scatter.2.cloned.1.call-done = bf16[128,4096]{1,0:T(8,128)(2,1)} async-done(((bf16[1024,4096]{1,0:T(8,128)(2,1)}), bf16[128,4096]{1,0:T(8,128)(2,1)}) %reduce-scatter.2.cloned.1.call-update) | async-done | bytes 1048592 | tf_op jit(solution)/shard_map/reduce_scatter | solution.py:144
  168.5 1.7 multiply_reduce_fusion.2
  170.3 0.6 multiply_reduce_fusion.1
  170.9 0.8 multiply_reduce_fusion
  171.7 0.2 copy.90
  172.0 1.4 copy.77
  173.3 2.9 all-to-all-start.1
  176.4 0.1 copy.78
  176.5 0.6 pad.11
  177.1 26.2 %all-to-all-done.1 = bf16[32,128,128]{2,1,0:T(8,128)(2,1)S(1)} async-done(((bf16[32,128,128]{2,1,0:T(8,128)(2,1)}), bf16[32,128,128]{2,1,0:T(8,128)(2,1)S(1)}, u32[]{:S(2)}, u32[]{:S(2)}) %all-to-all-start.1) | async-done | bytes 1048608 | tf_op jit(solution)/shard_map/all_to_all | solution.py:159
  203.4 32.2 %all-gather.7.cloned.1.call-done.name_ref = s32[2048,128]{1,0:T(8,128)} async-done(((s32[64,128]{1,0:T(8,128)}), s32[2048,128]{1,0:T(8,128)}) %all-gather.7.cloned.1.call-update) | async-done | bytes 1048592 | tf_op jit(solution)/shard_map/all_gather | solution.py:139
  235.6 1.2 copy-done.1
  236.8 12.2 %shard_map.85 = f32[2048,128]{1,0:T(8,128)S(1)} custom-call(bf16[2048,128]{1,0:T(8,128)(2,1)S(1)} %bitcast.101, bf16[2048,128]{1,0:T(8,128)(2,1)S(1)} %bitcast.97, s32[2048,128]{1,0:T(8,128)S(1)} %copy-done.1), custom_call_target="tpu_custom_call" | custom-call | tf_op jit(solution)/shard_map/pallas_call | solution.py:54
  249.0 1.9 all_to_all.30
  250.9 3.6 all-to-all-start.2
  254.5 0.3 fusion.13
  255.3 0.1 copy.82
  255.4 0.8 gather_fusion
  256.2 5.8 all-to-all-done.2
  262.1 0.1 reshape.120
  262.2 0.2 exponential_reduce_fusion
  262.4 0.2 fusion.21
  262.7 0.1 copy.83
  262.9 0.1 copy.85
  263.0 0.1 concatenate.19
  263.1 0.6 pad.12
  263.8 0.5 all-gather.13.cloned.1.call-update
  264.4 0.2 all-gather.11.cloned.1.call-start
  264.7 49.7 %all-gather.9.cloned.1.call-done.pack_ref = f32[2048,128]{1,0:T(8,128)} async-done(((f32[64,128]{1,0:T(8,128)}), f32[2048,128]{1,0:T(8,128)}) %all-gather.9.cloned.1.call-update) | async-done | bytes 1048592 | tf_op jit(solution)/shard_map/all_gather | solution.py:185
  314.4 1.2 copy-done
  315.6 29.7 %shard_map.86 = (f32[2048,128]{1,0:T(8,128)S(1)}, f32[2048,128]{1,0:T(8,128)S(1)}, f32[1,2048]{1,0:T(1,128)S(1)}) custom-call(bf16[2048,128]{1,0:T(8,128)(2,1)S(1)} %bitcast.102, bf16[2048,128]{1,0:T(8,128)(2,1)S(1)} %bitcast.98, s32[2048,128]{1,0:T(8,128)S(1)} %copy-done.2, f32[2048,128]{1,0:T(8,128)S(1)} %copy-done), custom_call_target="tpu_custom_call" | custom-call | tf_op jit(solution)/shard_map/pallas_call | solution.py:104
  345.4 4.8 slice_reduce_fusion.7
  350.3 1.4 fusion.12
  351.7 3.4 fusion.11
  355.1 0.3 all-gather.15.cloned.1.call-start
  355.4 47.2 %all-gather.13.cloned.1.call-done = bf16[4,1024,1024]{2,1,0:T(8,128)(2,1)} async-done(((bf16[1,1024,1024]{2,1,0:T(8,128)(2,1)}), bf16[4,1024,1024]{2,1,0:T(8,128)(2,1)}) %all-gather.13.cloned.1.call-update) | async-done | bytes 8388624 | tf_op jit(solution)/shard_map/all_gather | solution.py:147
  402.6 8.6 %copy.86 = bf16[2,8,4,64,1024]{4,3,2,1,0:T(8,128)(2,1)} copy(bf16[2,8,4,64,1024]{4,3,0,1,2:T(8,128)(2,1)} %bitcast.108) | data formatting | bytes 16777216 | tf_op jit(solution)/shard_map/transpose | solution.py:149
  411.1 75.4 %all-gather.11.cloned.1.call-done = bf16[4096,1024]{1,0:T(8,128)(2,1)} async-done(((bf16[4096,128]{1,0:T(8,128)(2,1)}), bf16[4096,1024]{1,0:T(8,128)(2,1)}) %all-gather.11.cloned.1.call-update) | async-done | bytes 8388624 | tf_op jit(solution)/shard_map/all_gather | solution.py:210
  486.5 14.8 %convert_bitcast_fusion = bf16[1024,1024]{0,1:T(8,128)(2,1)} fusion(bf16[4096,1024]{1,0:T(8,128)(2,1)} %all-gather.11.cloned.1.call-done, bf16[4096,1024]{1,0:T(8,128)(2,1)} %bitcast.109), kind=kOutput, calls=%fused_computation.19 | convolution fusion | flops 8590983168 | bytes 18874368 | tf_op jit(solution)/shard_map/dot_general | solution.py:211
  501.4 65.1 %all-gather = f32[32,1,128]{2,1,0:T(1,128)S(1)} all-gather(f32[1,1,128]{2,1,0:T(1,128)S(1)} %bitcast.136), channel_id=1, replica_groups=mesh['shard'=8,'replica'=4] {'shard','replica'}, dimensions={0}, use_global_device_ids=true | all-gather | bytes 16896 | tf_op jit(solution)/shard_map/all_gather | solution.py:207
  566.5 0.6 copy.96
  567.8 19.5 %all-gather.15.cloned.1.call-done = bf16[1024,4096]{0,1:T(8,128)(2,1)} async-done(((bf16[1024,1024]{0,1:T(8,128)(2,1)}), bf16[1024,4096]{0,1:T(8,128)(2,1)}) %all-gather.15.cloned.1.call-update) | async-done | bytes 8388624 | tf_op jit(solution)/shard_map/all_gather | solution.py:214
  587.3 12.3 %copy.88 = f32[1024,4096]{1,0:T(8,128)} copy(bf16[1024,4096]{0,1:T(8,128)(2,1)} %all-gather.15.cloned.1.call-done) | data formatting | bytes 25165824
  (49 shorter events, 1.3 us)
Async XLA Ops:
  8.0 160.5 %reduce-scatter.2.cloned.1.call-start = ((), (), s32[]{:S(2)}) async-start(), calls=%async_computation.4 | async-start | bytes 9437184 | tf_op jit(solution)/shard_map/reduce_scatter | solution.py:144
  11.0 58.0 %copy-start.9 = (bf16[1024,4096]{1,0:T(8,128)(2,1)S(1)}, bf16[1024,4096]{1,0:T(8,128)(2,1)}, u32[]{:S(2)}) copy-start(bf16[1024,4096]{1,0:T(8,128)(2,1)} %param.8) | copy-start | bytes 25165828
  67.7 1.4 copy-start.5
  79.8 88.7 %copy-start.3 = (bf16[2,64,4096]{2,1,0:T(8,128)(2,1)S(1)}, bf16[2,64,4096]{2,1,0:T(8,128)(2,1)}, u32[]{:S(2)}) copy-start(bf16[2,64,4096]{2,1,0:T(8,128)(2,1)} %param.7) | copy-start | bytes 3145732
  79.9 90.4 %copy-start.6 = (f32[4096]{0:T(1024)S(1)}, f32[4096]{0:T(1024)}, u32[]{:S(2)}) copy-start(f32[4096]{0:T(1024)} %param.9) | copy-start | bytes 49156
  168.5 1.8 copy-start.4
  171.9 4.4 copy-start.7
  171.9 4.4 copy-start.8
  173.3 30.0 %all-to-all-start.1 = ((bf16[32,128,128]{2,1,0:T(8,128)(2,1)}), bf16[32,128,128]{2,1,0:T(8,128)(2,1)S(1)}, u32[]{:S(2)}, u32[]{:S(2)}) async-start(bf16[32,128,128]{2,1,0:T(8,128)(2,1)} %bitcast.4), calls=%async_computation.2 | async-start | bytes 2097152 | tf_op jit(solution)/shard_map/all_to_all | solution.py:159
  176.3 59.3 %all-gather.7.cloned.1.call-start = ((), (), s32[]{:S(2)}) async-start(), calls=%async_computation.5 | async-start | bytes 1081344 | tf_op jit(solution)/shard_map/all_gather | solution.py:139
  235.6 1.2 copy-start.1
  250.9 11.1 %all-to-all-start.2 = ((f32[32,1,448]{2,1,0:T(1,128)}), f32[32,1,448]{2,1,0:T(1,128)S(1)}, u32[]{:S(2)}, u32[]{:S(2)}) async-start(f32[32,1,448]{2,1,0:T(1,128)} %all_to_all.30), calls=%async_computation.3 | async-start | bytes 131072 | tf_op jit(solution)/shard_map/all_to_all | solution.py:165
  254.5 59.9 %all-gather.9.cloned.1.call-start = ((), (), s32[]{:S(2)}) async-start(), calls=%async_computation.6 | async-start | bytes 1081344 | tf_op jit(solution)/shard_map/all_gather | solution.py:185
  254.8 59.6 %copy-start.2 = (s32[2048,128]{1,0:T(8,128)S(1)}, s32[2048,128]{1,0:T(8,128)}, u32[]{:S(2)}) copy-start(s32[2048,128]{1,0:T(8,128)} %all-gather.7.cloned.1.call-done.name_ref) | copy-start | bytes 3145732
  263.8 138.8 %all-gather.13.cloned.1.call-start = ((), (), s32[]{:S(2)}) async-start(), calls=%async_computation.8 | async-start | bytes 10485760 | tf_op jit(solution)/shard_map/all_gather | solution.py:147
  264.4 222.2 %all-gather.11.cloned.1.call-start = ((), (), s32[]{:S(2)}) async-start(), calls=%async_computation.7 | async-start | bytes 9437184 | tf_op jit(solution)/shard_map/all_gather | solution.py:210
  314.4 1.2 copy-start
  355.1 232.1 %all-gather.15.cloned.1.call-start = ((), (), s32[]{:S(2)}) async-start(), calls=%async_computation.9 | async-start | bytes 10485760 | tf_op jit(solution)/shard_map/all_gather | solution.py:214
Sparse Core Ops, SparseCore 0:
  80.0 88.5 reduce-scatter.1
Sparse Core Ops, SparseCore 1:
  179.8 55.8 all-gather.6
  263.9 50.5 all-gather.8
  316.1 86.4 all-gather.12
  404.2 82.3 all-gather.10
  501.4 85.8 all-gather.14

commit v2 on v1

--- a/solution.py
+++ b/solution.py
@@ -21,6 +21,15 @@
     scaled = normed * norm_gain
     length = jnp.sqrt(jnp.sum(scaled * scaled, axis=-1, keepdims=True))
     return (inv_rms, length, scaled / length)
+
+
+def three_parts(values):
+    parts = []
+    for _ in range(3):
+        part = lax.reduce_precision(values, 8, 7)
+        parts.append(part.astype(jnp.bfloat16))
+        values = values - part
+    return parts
 
 
 def softmax_terms(local_score, hard_score):
@@ -135,16 +144,15 @@
     total = count * devices
     block = 256 if total <= 2048 else 64
 
-    name = jnp.pad(hard_owner * count + hard_row, ((0, 0), (0, LANES - HARD)))
-    names = lax.all_gather(name, everywhere, axis=0, tiled=True)
-
     rows = activations.reshape(2 * count, activations.shape[2])
     spread_rows = lax.all_to_all(rows, "shard", split_axis=1, concat_axis=0, tiled=True)
     terms = jnp.dot(spread_rows, down_weight, preferred_element_type=jnp.float32)
     mixed = lax.psum_scatter(
         terms.astype(jnp.bfloat16), "shard", scatter_dimension=0, tiled=True
-    ).astype(jnp.float32)
+    )
     all_rows = lax.all_gather(spread_rows, "replica", axis=0, tiled=False)
+    mixed, all_rows = lax.optimization_barrier((mixed, all_rows))
+    mixed = mixed.astype(jnp.float32)
     all_rows = all_rows.reshape(n_replica, n_shard, 2, count, hidden)
     all_rows = all_rows.transpose(2, 1, 0, 3, 4).reshape(2 * total, hidden)
 
@@ -156,9 +164,19 @@
 
     cut = unit.reshape(2 * count, n_replica, n_shard, feats).transpose(2, 1, 0, 3)
     cut = cut.reshape(devices, 2 * count, feats)
+    name = jnp.concatenate([hard_owner.T, hard_row.T]).astype(jnp.bfloat16).reshape(-1)
+    taken = name.shape[0]
+    extra_rows = -(-taken // (16 * feats)) * 16
+    name = jnp.pad(name, (0, extra_rows * feats - taken)).reshape(1, extra_rows, feats)
+    name = jnp.broadcast_to(name, (devices, extra_rows, feats))
+    cut = jnp.concatenate([cut, name], axis=1)
     cut = lax.all_to_all(cut, everywhere, split_axis=0, concat_axis=0, tiled=True)
     queries = cut[:, :count].reshape(total, feats)
-    passages = cut[:, count:].reshape(total, feats)
+    passages = cut[:, count : 2 * count].reshape(total, feats)
+    name = cut[:, 2 * count :].reshape(devices, -1)[:, :taken].astype(jnp.int32)
+    name = name.reshape(devices, 2, HARD, count)
+    names = (name[:, 0] * count + name[:, 1]).transpose(0, 2, 1).reshape(total, HARD)
+    names = jnp.pad(names, ((0, 0), (0, LANES - HARD)))
 
     local_score = jnp.dot(unit[:count], unit[count:].T, preferred_element_type=jnp.float32)
     partial = pick_scores(queries, passages, names, block)[:, :HARD]
@@ -168,9 +186,8 @@
     hard_score = jnp.sum(partial, axis=0).reshape(count, HARD)
     losses, weights, shares = softmax_terms(local_score, hard_score)
 
-    pack = jnp.concatenate(
+    scalars = jnp.concatenate(
         [
-            weights,
             shares[:, count:],
             jnp.sum(shares, axis=1, keepdims=True),
             jnp.sum(shares[:, :count], axis=0)[:, None],
@@ -181,8 +198,15 @@
         ],
         axis=1,
     )
+    pack = jnp.concatenate([weights.astype(jnp.bfloat16), *three_parts(scalars)], axis=1)
     pack = jnp.pad(pack, ((0, 0), (0, LANES - pack.shape[1])))
-    pack = lax.all_gather(pack, everywhere, axis=0, tiled=True)
+    pack = jnp.broadcast_to(pack, (devices, count, LANES))
+    pack = lax.all_to_all(pack, everywhere, split_axis=0, concat_axis=0, tiled=True)
+    pack = pack.reshape(total, LANES).astype(jnp.float32)
+    first, some = count + HARD, scalars.shape[1]
+    scalars = sum(pack[:, first + part * some : first + (part + 1) * some] for part in range(3))
+    pack = jnp.concatenate([pack[:, :first], scalars], axis=1)
+    pack = jnp.pad(pack, ((0, 0), (0, LANES - pack.shape[1])))
     at = count + 2 * HARD
 
     def both(first):
@@ -204,16 +228,17 @@
     grad_stream = inv_rms * (grad_scaled * gain - normed * mean)
     grad_stream = grad_stream.astype(jnp.bfloat16).reshape(2 * total, feats)
 
-    gain_grad = lax.all_gather(gain_part, everywhere, axis=0, tiled=True)
-    gain_grad = gain_grad.reshape(n_shard, n_replica, feats).transpose(1, 0, 2).reshape(width)
-
-    columns = lax.all_gather(grad_stream, "shard", axis=1, tiled=True)
+    extra = jnp.pad(jnp.stack(three_parts(gain_part)), ((0, 13), (0, 0)))
+    columns = lax.all_gather(
+        jnp.concatenate([grad_stream, extra], axis=0), "shard", axis=1, tiled=True
+    )
     quarter = lax.dot_general(
-        all_rows, columns, (((0,), (0,)), ((), ())), preferred_element_type=jnp.float32
-    )
-    weight_grad = lax.all_gather(
-        quarter.astype(jnp.bfloat16), "replica", axis=1, tiled=True
-    ).astype(jnp.float32)
+        all_rows, columns[: 2 * total], (((0,), (0,)), ((), ())), preferred_element_type=jnp.float32
+    )
+    quarter = jnp.concatenate([quarter.astype(jnp.bfloat16), columns[2 * total :]], axis=0)
+    gathered = lax.all_gather(quarter, "replica", axis=1, tiled=True).astype(jnp.float32)
+    weight_grad = gathered[:hidden]
+    gain_grad = jnp.sum(gathered[hidden : hidden + 3], axis=0)
     return (mean_loss, weight_grad, gain_grad)
 
 

time: 609 us -> 514 us (0.84)
  blocking collectives: 121 us -> 55.3 us
  waiting for transfers between devices: 345 us -> 295 us
  other arithmetic: 13.3 us -> 30.5 us
    reduce_scatter x1, waiting for transfers between devices: 88.7 us -> 17.6 us  [per_device(): lax.psum_scatter(terms.astype(jnp.bfloat16), 'shard', scatter_dimension=0...]
    all_gather x1 -> x0, blocking collectives: 65.1 us -> none  [per_device(): gain_grad = lax.all_gather(gain_part, everywhere, axis=0, tiled=True)]
    all_gather x1, waiting for transfers between devices: 47.2 us -> 70.1 us  [per_device(): all_rows = lax.all_gather(spread_rows, 'replica', axis=0, tiled=False)]
    all_gather x4 -> x2, waiting for transfers between devices: 177 us -> 158 us  [the longest x1 86.4 us: per_device(): lax.all_gather(quarter, 'replica', axis=1, tiled=True).astype(jnp.float32)]
    all_to_all x0 -> x1, waiting for transfers between devices: none -> 16.1 us  [per_device(): lax.all_to_all(pack, everywhere, split_axis=0, concat_axis=0, tiled=True)]
    unnamed x27 -> x22, local copies, waits for them, and re-layouts: 19.4 us -> 5.9 us
    slice x1 -> x5, local copies, waits for them, and re-layouts: 0.08 us -> 12 us  [the longest x1 11.8 us: per_device(): weight_grad = gathered[:hidden]]
    convert_element_type x0 -> x4, other arithmetic: none -> 11.7 us  [the longest x1 11.5 us: per_device(): lax.all_gather(quarter, 'replica', axis=1, tiled=True).astype(jnp.float32)]
  transfers between devices with their start and end apart: 8 -> 7, of which waited for: 8 -> 7; matrix products, arithmetic and copies ran while one was open for 4% -> 5% of each run, Pallas kernels for 5% -> 0%
where the time goes in v2:
time: 514 us; the launch traced here: 513 us
  waiting for transfers between devices  295 us (57%)
  blocking collectives  55.3 us (11%)
  Pallas kernels  42 us (8%)
  local copies, waits for them, and re-layouts  33 us (6%)
  other arithmetic  30.5 us (6%)
  matrix products  29.4 us (6%)
  between operations  17.6 us (3%)
  starting transfers between devices  9.8 us (2%)
    all_gather x1, waiting for transfers between devices, per_device(): lax.all_gather(quarter, 'replica', axis=1, tiled=True).astype(jnp.float32)  86.4 us
    all_gather x1, waiting for transfers between devices, per_device(): lax.all_gather(jnp.concatenate([grad_stream, extra], axis=0), 'shard', ax...  71.5 us
    all_gather x1, waiting for transfers between devices, per_device(): all_rows = lax.all_gather(spread_rows, 'replica', axis=0, tiled=False)  70.1 us
    all_to_all x1, blocking collectives, per_device(): lax.all_to_all(rows, 'shard', split_axis=1, concat_axis=0, tiled=True)  55.3 us
    pallas_call x1, Pallas kernels, spread_grads(): pl.pallas_call(functools.partial(spread_kernel, group_rows), grid=(total...  29.7 us
    all_to_all x1, waiting for transfers between devices, per_device(): lax.all_to_all(cut, everywhere, split_axis=0, concat_axis=0, tiled=True)  29.1 us
    reduce_scatter x1, waiting for transfers between devices, per_device(): lax.psum_scatter(terms.astype(jnp.bfloat16), 'shard', scatter_dimension=0...  17.6 us
    all_to_all x1, waiting for transfers between devices, per_device(): lax.all_to_all(pack, everywhere, split_axis=0, concat_axis=0, tiled=True)  16.1 us
  transfers between devices with their start and end apart: 7, of which 7 were waited for; matrix products, arithmetic and copies ran while one was open for 5% of the time, Pallas kernels for 0%

profile of v2, /device:TPU:0, one launch (start us, length us, event | category | flops | bytes accessed | tf_op | source)
XLA Modules:
  0.0 513.1 jit_solution(2185601602613117802)
XLA Ops:
  8.0 3.0 copy.71
  11.0 1.2 copy.62
  12.2 55.3 %all_to_all.39 = bf16[128,8,1024]{2,0,1:T(8,128)(2,1)} all-to-all(bf16[128,8,1024]{2,0,1:T(8,128)(2,1)S(1)} %copy.62), channel_id=1, replica_groups=mesh['shard'=8,'replica'=4] {'shard'}, dimensions={1} | all-to-all | bytes 4194304 | tf_op jit(solution)/shard_map/all_to_all | solution.py:148
  67.6 1.5 copy-done.2
  69.1 14.2 %convolution_convert_fusion = bf16[1024,4096]{1,0:T(8,128)(2,1)} fusion(bf16[1024,1024]{1,0:T(8,128)(2,1)S(1)} %bitcast.128, bf16[1024,4096]{1,0:T(8,128)(2,1)} %param.8), kind=kOutput, calls=%fused_computation.3 | convolution fusion | flops 8594128896 | bytes 18874368 | tf_op jit(solution)/shard_map/dot_general | solution.py:149
  83.3 0.7 copy-done.5
  84.1 70.1 %all-gather.4.cloned.1.call-done = bf16[4,1024,1024]{2,1,0:T(8,128)(2,1)} async-done(((bf16[1,1024,1024]{2,1,0:T(8,128)(2,1)}), bf16[4,1024,1024]{2,1,0:T(8,128)(2,1)}) %all-gather.4.cloned.1.call-update) | async-done | bytes 8388624 | tf_op jit(solution)/shard_map/all_gather | solution.py:153
  154.2 17.6 %reduce-scatter.2.cloned.1.call-done = bf16[128,4096]{1,0:T(8,128)(2,1)} async-done(((bf16[1024,4096]{1,0:T(8,128)(2,1)}), bf16[128,4096]{1,0:T(8,128)(2,1)}) %reduce-scatter.2.cloned.1.call-update) | async-done | bytes 1048592 | tf_op jit(solution)/shard_map/reduce_scatter | solution.py:150
  171.8 1.7 multiply_reduce_fusion.2
  173.5 0.6 multiply_reduce_fusion.1
  174.1 0.8 multiply_reduce_fusion
  174.9 0.2 copy.72
  175.2 0.4 copy.63
  175.6 0.3 copy-done.3
  175.9 1.1 pad_maximum_fusion.1
  177.0 3.1 all-to-all-start.1
  180.1 29.1 %all-to-all-done.1 = bf16[32,144,128]{2,1,0:T(8,128)(2,1)S(1)} async-done(((bf16[32,144,128]{2,1,0:T(8,128)(2,1)}), bf16[32,144,128]{2,1,0:T(8,128)(2,1)S(1)}, u32[]{:S(2)}, u32[]{:S(2)}) %all-to-all-start.1) | async-done | bytes 1179680 | tf_op jit(solution)/shard_map/all_to_all | solution.py:173
  209.3 0.1 reshape.182
  209.4 0.4 copy.64
  209.9 0.1 fusion.35
  210.0 12.2 %shard_map.85 = f32[2048,128]{1,0:T(8,128)S(1)} custom-call(bf16[2048,128]{1,0:T(8,128)(2,1)S(1)} %bitcast.117, bf16[2048,128]{1,0:T(8,128)(2,1)S(1)} %bitcast.113, s32[2048,128]{1,0:T(8,128)S(1)} %pad.24.name_ref), custom_call_target="tpu_custom_call" | custom-call | tf_op jit(solution)/shard_map/pallas_call | solution.py:63
  222.3 1.9 all_to_all.34
  224.1 3.7 all-to-all-start.2
  227.9 1.5 fusion.18
  229.6 0.8 gather_fusion
  230.5 4.7 all-to-all-done.2
  235.3 0.1 reshape.177
  235.6 0.1 slice_reduce_fusion.10
  235.9 0.9 broadcast_in_dim.18
  236.8 2.6 all-to-all-start.3
  239.6 16.1 %all-to-all-done.3 = bf16[32,64,128]{2,1,0:T(8,128)(2,1)S(1)} async-done(((bf16[32,64,128]{2,1,0:T(8,128)(2,1)}), bf16[32,64,128]{2,1,0:T(8,128)(2,1)S(1)}, u32[]{:S(2)}, u32[]{:S(2)}) %all-to-all-start.3) | async-done | bytes 524320 | tf_op jit(solution)/shard_map/all_to_all | solution.py:204
  255.7 0.1 bitcast_convert_fusion
  255.8 0.9 slice_add_fusion
  256.7 4.8 slice_reduce_fusion.7
  261.5 0.3 select_maximum_fusion.pack_ref
  261.8 29.7 %shard_map.86 = (f32[2048,128]{1,0:T(8,128)S(1)}, f32[2048,128]{1,0:T(8,128)S(1)}, f32[1,2048]{1,0:T(1,128)S(1)}) custom-call(bf16[2048,128]{1,0:T(8,128)(2,1)S(1)} %bitcast.118, bf16[2048,128]{1,0:T(8,128)(2,1)S(1)} %bitcast.114, s32[2048,128]{1,0:T(8,128)S(1)} %pad.24.name_ref, f32[2048,128]{1,0:T(8,128)S(1)} %select_maximum_fusion.pack_ref), custom_call_target="tpu_custom_call" | custom-call | tf_op jit(solution)/shard_map/pallas_call | solution.py:113
  291.7 1.4 maximum_multiply_fusion
  293.1 2.6 fusion.13
  295.8 1.1 pad_maximum_fusion.2
  296.9 0.3 all-gather.8.cloned.1.call-start
  297.1 8.6 %copy.69 = bf16[2,8,4,64,1024]{4,3,2,1,0:T(8,128)(2,1)} copy(bf16[2,8,4,64,1024]{4,3,0,1,2:T(8,128)(2,1)} %bitcast.125) | data formatting | bytes 16777216 | tf_op jit(solution)/shard_map/transpose | solution.py:157
  305.8 71.5 %all-gather.6.cloned.1.call-done = bf16[4112,1024]{1,0:T(8,128)(2,1)} async-done(((bf16[4112,128]{1,0:T(8,128)(2,1)}), bf16[4112,1024]{1,0:T(8,128)(2,1)}) %all-gather.6.cloned.1.call-update) | async-done | bytes 8421392 | tf_op jit(solution)/shard_map/all_gather | solution.py:232
  377.3 13.7 %fusion.15 = bf16[1024,1024]{1,0:T(8,128)(2,1)S(1)} fusion(bf16[4096,1024]{1,0:T(8,128)(2,1)} %bitcast.126, bf16[4112,1024]{1,0:T(8,128)(2,1)} %all-gather.6.cloned.1.call-done), kind=kOutput, calls=%fused_computation.29 | convolution fusion | flops 8590983168 | bytes 18874368 | tf_op jit(solution)/shard_map/dot_general | solution.py:235
  391.0 1.5 pad_maximum_fusion
  393.2 86.4 %all-gather.8.cloned.1.call-done = bf16[1040,4096]{1,0:T(8,128)(2,1)} async-done(((bf16[1040,1024]{1,0:T(8,128)(2,1)}), bf16[1040,4096]{1,0:T(8,128)(2,1)}) %all-gather.8.cloned.1.call-update) | async-done | bytes 8519696 | tf_op jit(solution)/shard_map/all_gather | solution.py:239
  479.6 11.5 %convert_element_type.126 = f32[1040,4096]{1,0:T(8,128)} convert(bf16[1040,4096]{1,0:T(8,128)(2,1)} %all-gather.8.cloned.1.call-done) | non-fusion elementwise | flops 4259840 | bytes 25559040 | tf_op jit(solution)/shard_map/convert_element_type | solution.py:239
  491.2 1.5 slice_reduce_fusion.9
  492.7 11.8 %slice.158 = f32[1024,4096]{1,0:T(8,128)} slice(bf16[1040,4096]{1,0:T(8,128)(2,1)} %all-gather.8.cloned.1.call-done), slice={[0:1024], [0:4096]} | slice | bytes 33554432 | tf_op jit(solution)/shard_map/slice | solution.py:240
  (59 shorter events, 1.5 us)
Async XLA Ops:
  8.0 146.2 %all-gather.4.cloned.1.call-start = ((), (), s32[]{:S(2)}) async-start(), calls=%async_computation.6 | async-start | bytes 10485760 | tf_op jit(solution)/shard_map/all_gather | solution.py:153
  67.5 1.6 copy-start.2
  67.5 104.2 %reduce-scatter.2.cloned.1.call-start = ((), (), s32[]{:S(2)}) async-start(), calls=%async_computation.5 | async-start | bytes 9437184 | tf_op jit(solution)/shard_map/reduce_scatter | solution.py:150
  83.3 0.7 copy-start.5
  83.3 0.7 copy-start.6
  83.3 88.5 %copy-start = (bf16[2,64,4096]{2,1,0:T(8,128)(2,1)S(1)}, bf16[2,64,4096]{2,1,0:T(8,128)(2,1)}, u32[]{:S(2)}) copy-start(bf16[2,64,4096]{2,1,0:T(8,128)(2,1)} %param.7) | copy-start | bytes 3145732
  84.0 89.5 %copy-start.4 = (f32[4096]{0:T(1024)S(1)}, f32[4096]{0:T(1024)}, u32[]{:S(2)}) copy-start(f32[4096]{0:T(1024)} %param.9) | copy-start | bytes 49156
  171.8 1.8 copy-start.1
  174.9 1.0 copy-start.3
  177.0 32.2 %all-to-all-start.1 = ((bf16[32,144,128]{2,1,0:T(8,128)(2,1)}), bf16[32,144,128]{2,1,0:T(8,128)(2,1)S(1)}, u32[]{:S(2)}, u32[]{:S(2)}) async-start(bf16[32,144,128]{2,1,0:T(8,128)(2,1)} %pad_maximum_fusion.1), calls=%async_computation.2 | async-start | bytes 2359296 | tf_op jit(solution)/shard_map/all_to_all | solution.py:173
  224.1 11.1 %all-to-all-start.2 = ((f32[32,1,448]{2,1,0:T(1,128)}), f32[32,1,448]{2,1,0:T(1,128)S(1)}, u32[]{:S(2)}, u32[]{:S(2)}) async-start(f32[32,1,448]{2,1,0:T(1,128)} %all_to_all.34), calls=%async_computation.3 | async-start | bytes 131072 | tf_op jit(solution)/shard_map/all_to_all | solution.py:183
  236.8 18.9 %all-to-all-start.3 = ((bf16[32,64,128]{2,1,0:T(8,128)(2,1)}), bf16[32,64,128]{2,1,0:T(8,128)(2,1)S(1)}, u32[]{:S(2)}, u32[]{:S(2)}) async-start(bf16[32,64,128]{2,1,0:T(8,128)(2,1)} %broadcast_in_dim.18), calls=%async_computation.4 | async-start | bytes 1048576 | tf_op jit(solution)/shard_map/all_to_all | solution.py:204
  239.4 137.8 %all-gather.6.cloned.1.call-start = ((), (), s32[]{:S(2)}) async-start(), calls=%async_computation.7 | async-start | bytes 9474048 | tf_op jit(solution)/shard_map/all_gather | solution.py:232
  296.9 182.7 %all-gather.8.cloned.1.call-start = ((), (), s32[]{:S(2)}) async-start(), calls=%async_computation.8 | async-start | bytes 10649600 | tf_op jit(solution)/shard_map/all_gather | solution.py:239
  377.3 13.8 %slice-start = ((bf16[4112,1024]{1,0:T(8,128)(2,1)}), bf16[16,1024]{1,0:T(8,128)(2,1)S(1)}, s32[]{:S(2)}) async-start(bf16[4112,1024]{1,0:T(8,128)(2,1)} %all-gather.6.cloned.1.call-done), calls=%async_computation.9 | async-start | bytes 65536 | tf_op jit(solution)/shard_map/slice | solution.py:238
Sparse Core Ops, SparseCore 0:
  67.6 86.5 all-gather.3
  392.7 86.8 all-gather.7
Sparse Core Ops, SparseCore 1:
  83.4 88.3 reduce-scatter.1
  297.0 80.3 all-gather.5

commit v3 on v2

--- a/solution.py
+++ b/solution.py
@@ -9,6 +9,7 @@
 
 HARD = 7
 LANES = 128
+PIECES = 2
 
 
 epsilon = 1e-05
@@ -74,7 +75,9 @@
     )(queries, passages, names)
 
 
-def spread_kernel(group_rows, q_ref, p_ref, name_ref, pack_ref, gq_ref, gp_ref, tp_ref):
+def spread_kernel(
+    group_rows, q_ref, p_ref, name_ref, pack_ref, widen_ref, gq_ref, gp_ref, tp_ref
+):
     step = pl.program_id(0)
 
     @pl.when(step == 0)
@@ -83,17 +86,28 @@
         tp_ref[...] = jnp.zeros_like(tp_ref)
 
     block, total = q_ref.shape[0], p_ref.shape[0]
-    column = lax.broadcasted_iota(jnp.int32, (block, total), 1)
-    weight = jnp.zeros((block, total), jnp.float32)
-    share = jnp.zeros((block, total), jnp.float32)
+    name = name_ref[...]
+    owner, row = name // group_rows, (name % group_rows).astype(jnp.float32)
+    lane = lax.broadcasted_iota(jnp.int32, (block, LANES), 1)
+    rows = jnp.full((block, LANES), -1.0, jnp.float32)
+    weight = jnp.zeros((block, LANES), jnp.float32)
+    share = jnp.zeros((block, LANES), jnp.float32)
     for k in range(HARD):
-        hit = column == name_ref[:, k : k + 1]
-        weight = jnp.where(hit, pack_ref[:, group_rows + k : group_rows + k + 1], weight)
-        share = jnp.where(
-            hit, pack_ref[:, group_rows + HARD + k : group_rows + HARD + k + 1], share
+        hit = lane == owner[:, k : k + 1]
+        at = group_rows + k
+        rows = jnp.where(hit, row[:, k : k + 1], rows)
+        weight = jnp.where(hit, pack_ref[:, at : at + 1], weight)
+        share = jnp.where(hit, pack_ref[:, at + HARD : at + HARD + 1], share)
+
+    def widen(values):
+        return jnp.dot(
+            values.astype(jnp.bfloat16), widen_ref[...], preferred_element_type=jnp.float32
         )
-    tp_ref[...] += jnp.sum(share, axis=0, keepdims=True)
-    weight = weight.astype(jnp.bfloat16)
+
+    column = lax.broadcasted_iota(jnp.int32, (1, total), 1) % group_rows
+    hit = widen(rows) == column.astype(jnp.float32)
+    tp_ref[...] += jnp.sum(jnp.where(hit, widen(share), 0.0), axis=0, keepdims=True)
+    weight = jnp.where(hit, widen(weight), 0.0).astype(jnp.bfloat16)
     gq_ref[...] = jnp.dot(weight, p_ref[...], preferred_element_type=jnp.float32)
     gp_ref[...] += lax.dot_general(
         weight, q_ref[...], (((0,), (0,)), ((), ())), preferred_element_type=jnp.float32
@@ -110,6 +124,8 @@
 
 def spread_grads(queries, passages, names, pack, block, group_rows):
     total, feats = queries.shape
+    owner = jnp.arange(total, dtype=jnp.int32)[None, :] // group_rows
+    widen = (jnp.arange(LANES, dtype=jnp.int32)[:, None] == owner).astype(jnp.bfloat16)
     return pl.pallas_call(
         functools.partial(spread_kernel, group_rows),
         grid=(total // block,),
@@ -118,6 +134,7 @@
             pl.BlockSpec((total, feats), lambda i: (0, 0)),
             pl.BlockSpec((block, LANES), lambda i: (i, 0)),
             pl.BlockSpec((block, LANES), lambda i: (i, 0)),
+            pl.BlockSpec((LANES, total), lambda i: (0, 0)),
         ],
         out_specs=[
             pl.BlockSpec((block, feats), lambda i: (i, 0)),
@@ -130,7 +147,28 @@
             jax.ShapeDtypeStruct((1, total), jnp.float32),
         ],
         compiler_params=pltpu.CompilerParams(vmem_limit_bytes=48 * 1024 * 1024),
-    )(queries, passages, names, pack)
+    )(queries, passages, names, pack, widen)
+
+
+def lay_kernel(*refs):
+    *pieces, out_ref = refs
+    span = pieces[0].shape[2]
+    for at, piece in enumerate(pieces):
+        out_ref[:, at * span : (at + 1) * span] = piece[0].astype(jnp.float32)
+
+
+def lay_columns(pieces, hidden):
+    parts, _, span = pieces[0].shape
+    block = min(hidden, 256)
+    wide = span * len(pieces)
+    return pl.pallas_call(
+        lay_kernel,
+        grid=(parts, hidden // block),
+        in_specs=[pl.BlockSpec((1, block, span), lambda r, i: (r, i, 0)) for _ in pieces],
+        out_specs=pl.BlockSpec((block, wide), lambda r, i: (i, r)),
+        out_shape=jax.ShapeDtypeStruct((hidden, parts * wide), jnp.float32),
+        compiler_params=pltpu.CompilerParams(vmem_limit_bytes=32 * 1024 * 1024),
+    )(*pieces)
 
 
 def per_device(activations, residual, down_weight, norm_gain, hard_owner, hard_row):
@@ -162,7 +200,8 @@
     held = unit.astype(jnp.float32)
     square = jnp.sum(held * held, axis=-1, keepdims=True)
 
-    cut = unit.reshape(2 * count, n_replica, n_shard, feats).transpose(2, 1, 0, 3)
+    small = feats // PIECES
+    cut = unit.reshape(2 * count, n_replica, PIECES, n_shard, small).transpose(3, 1, 0, 2, 4)
     cut = cut.reshape(devices, 2 * count, feats)
     name = jnp.concatenate([hard_owner.T, hard_row.T]).astype(jnp.bfloat16).reshape(-1)
     taken = name.shape[0]
@@ -217,8 +256,10 @@
     inv_rms, length, square = both(at + 2), both(at + 4), both(at + 6)
     mean_loss = jnp.sum(pack[:, at + 8]) / total
 
-    start = lax.axis_index("replica") * (width // n_replica) + lax.axis_index("shard") * feats
-    gain = lax.dynamic_slice(norm_gain, (start,), (feats,))
+    gain = norm_gain.reshape(n_replica, PIECES, n_shard, small)
+    gain = lax.dynamic_index_in_dim(gain, lax.axis_index("replica"), 0, keepdims=False)
+    gain = lax.dynamic_index_in_dim(gain, lax.axis_index("shard"), 1, keepdims=False)
+    gain = gain.reshape(feats)
     held = jnp.stack([queries, passages]).astype(jnp.float32)
     grad_unit = jnp.stack([grad_q, grad_p]) / sharpness_divisor
     grad_scaled = (grad_unit - held * dots) / length
@@ -229,16 +270,22 @@
     grad_stream = grad_stream.astype(jnp.bfloat16).reshape(2 * total, feats)
 
     extra = jnp.pad(jnp.stack(three_parts(gain_part)), ((0, 13), (0, 0)))
-    columns = lax.all_gather(
-        jnp.concatenate([grad_stream, extra], axis=0), "shard", axis=1, tiled=True
-    )
-    quarter = lax.dot_general(
-        all_rows, columns[: 2 * total], (((0,), (0,)), ((), ())), preferred_element_type=jnp.float32
-    )
-    quarter = jnp.concatenate([quarter.astype(jnp.bfloat16), columns[2 * total :]], axis=0)
-    gathered = lax.all_gather(quarter, "replica", axis=1, tiled=True).astype(jnp.float32)
-    weight_grad = gathered[:hidden]
-    gain_grad = jnp.sum(gathered[hidden : hidden + 3], axis=0)
+    sent = jnp.concatenate([grad_stream, extra], axis=0).T
+    pieces = []
+    for piece in range(PIECES):
+        mine = sent[piece * small : (piece + 1) * small]
+        columns = lax.all_gather(mine, "shard", axis=0, tiled=True)
+        product = lax.dot_general(
+            all_rows,
+            columns[:, : 2 * total],
+            (((0,), (1,)), ((), ())),
+            preferred_element_type=jnp.float32,
+        ).astype(jnp.bfloat16)
+        product = jnp.concatenate([product, columns[:, 2 * total :].T], axis=0)
+        pieces.append(lax.all_gather(product, "replica", axis=0, tiled=False))
+    weight_grad = lay_columns(pieces, hidden)
+    gain_grad = jnp.stack([piece[:, hidden : hidden + 3] for piece in pieces], axis=1)
+    gain_grad = jnp.sum(gain_grad.astype(jnp.float32), axis=2).reshape(width)
     return (mean_loss, weight_grad, gain_grad)
 
 

time: 514 us -> 519 us (level)
  other arithmetic: 30.5 us -> 19 us
  waiting for transfers between devices: 295 us -> 303 us
  local copies, waits for them, and re-layouts: 33 us -> 40.1 us
    all_gather x2 -> x4, waiting for transfers between devices: 158 us -> 170 us  [the longest x2 96.7 us: per_device(): pieces.append(lax.all_gather(product, 'replica', axis=0, tiled=False))]
    pallas_call x1, Pallas kernels: 29.7 us -> 18.4 us  [spread_grads(): pl.pallas_call(functools.partial(spread_kernel, group_rows), grid=(total...]
    convert_element_type x1 -> x2, other arithmetic: 11.5 us -> 1.56 us  [the longest x1 1.46 us: per_device(): held = jnp.stack([queries, passages]).astype(jnp.float32)]
    slice x3, local copies, waits for them, and re-layouts: 11.8 us -> 2.9 us  [the longest x2 1.83 us: per_device(): product = jnp.concatenate([product, columns[:, 2 * total:].T], axis=0)]
    pallas_call x0 -> x1, Pallas kernels: none -> 8.64 us  [lay_columns(): pl.pallas_call(lay_kernel, grid=(parts, hidden // block), in_specs=[pl.Bl...]
    unnamed x22 -> x31, local copies, waits for them, and re-layouts: 5.9 us -> 11 us
    dot_general x1 -> x2, matrix products: 13.7 us -> 18.2 us  [per_device(): lax.dot_general(all_rows, columns[:, :2 * total], (((0,), (1,)), ((), ())...]
  transfers between devices with their start and end apart: 7 -> 9, of which waited for: 7 -> 9; matrix products, arithmetic and copies ran while one was open for 5% -> 10% of each run, Pallas kernels for 0% -> 0%
where the time goes in v3:
time: 519 us; the launch traced here: 518 us
  waiting for transfers between devices  303 us (58%)
  blocking collectives  55.3 us (11%)
  local copies, waits for them, and re-layouts  40.1 us (8%)
  Pallas kernels  39.3 us (8%)
  matrix products  33.9 us (7%)
  other arithmetic  19 us (4%)
  between operations  17.8 us (3%)
  starting transfers between devices  9.89 us (2%)
    all_gather x2, waiting for transfers between devices, per_device(): pieces.append(lax.all_gather(product, 'replica', axis=0, tiled=False))  96.7 us
    all_gather x2, waiting for transfers between devices, per_device(): columns = lax.all_gather(mine, 'shard', axis=0, tiled=True)  73.1 us
    all_gather x1, waiting for transfers between devices, per_device(): all_rows = lax.all_gather(spread_rows, 'replica', axis=0, tiled=False)  70 us
    all_to_all x1, blocking collectives, per_device(): lax.all_to_all(rows, 'shard', split_axis=1, concat_axis=0, tiled=True)  55.3 us
    all_to_all x1, waiting for transfers between devices, per_device(): lax.all_to_all(cut, everywhere, split_axis=0, concat_axis=0, tiled=True)  29.1 us
    pallas_call x1, Pallas kernels, spread_grads(): pl.pallas_call(functools.partial(spread_kernel, group_rows), grid=(total...  18.4 us
    dot_general x2, matrix products, per_device(): lax.dot_general(all_rows, columns[:, :2 * total], (((0,), (1,)), ((), ())...  18.2 us
    reduce_scatter x1, waiting for transfers between devices, per_device(): lax.psum_scatter(terms.astype(jnp.bfloat16), 'shard', scatter_dimension=0...  17.6 us
  transfers between devices with their start and end apart: 9, of which 9 were waited for; matrix products, arithmetic and copies ran while one was open for 10% of the time, Pallas kernels for 0%

profile of v3, /device:TPU:0, one launch (start us, length us, event | category | flops | bytes accessed | tf_op | source)
XLA Modules:
  0.0 518.5 jit_solution(15656640396781953064)
XLA Ops:
  8.0 3.0 copy.125
  11.0 1.2 copy.103
  12.2 55.3 %all_to_all.39 = bf16[128,8,1024]{2,0,1:T(8,128)(2,1)} all-to-all(bf16[128,8,1024]{2,0,1:T(8,128)(2,1)S(1)} %copy.103), channel_id=1, replica_groups=mesh['shard'=8,'replica'=4] {'shard'}, dimensions={1} | all-to-all | bytes 4194304 | tf_op jit(solution)/shard_map/all_to_all | solution.py:186
  67.6 1.5 copy-done.5
  69.1 14.2 %convolution_convert_fusion = bf16[1024,4096]{1,0:T(8,128)(2,1)} fusion(bf16[1024,1024]{1,0:T(8,128)(2,1)S(1)} %bitcast.123, bf16[1024,4096]{1,0:T(8,128)(2,1)} %param.8), kind=kOutput, calls=%fused_computation.1 | convolution fusion | flops 8594128896 | bytes 18874368 | tf_op jit(solution)/shard_map/dot_general | solution.py:187
  83.3 0.7 copy-done.8
  84.2 70.0 %all-gather.8.cloned.1.call-done = bf16[4,1024,1024]{2,1,0:T(8,128)(2,1)} async-done(((bf16[1,1024,1024]{2,1,0:T(8,128)(2,1)}), bf16[4,1024,1024]{2,1,0:T(8,128)(2,1)}) %all-gather.8.cloned.1.call-update) | async-done | bytes 8388624 | tf_op jit(solution)/shard_map/all_gather | solution.py:191
  154.2 17.6 %reduce-scatter.2.cloned.1.call-done = bf16[128,4096]{1,0:T(8,128)(2,1)} async-done(((bf16[1024,4096]{1,0:T(8,128)(2,1)}), bf16[128,4096]{1,0:T(8,128)(2,1)}) %reduce-scatter.2.cloned.1.call-update) | async-done | bytes 1048592 | tf_op jit(solution)/shard_map/reduce_scatter | solution.py:188
  171.8 1.7 multiply_reduce_fusion.3
  174.2 0.8 multiply_reduce_fusion.1
  174.9 0.7 copy.104
  176.8 2.7 copy.107
  179.4 3.1 all-to-all-start.1
  182.5 29.1 %all-to-all-done.1 = bf16[32,144,128]{2,1,0:T(8,128)(2,1)S(1)} async-done(((bf16[32,144,128]{2,1,0:T(8,128)(2,1)}), bf16[32,144,128]{2,1,0:T(8,128)(2,1)S(1)}, u32[]{:S(2)}, u32[]{:S(2)}) %all-to-all-start.1) | async-done | bytes 1179680 | tf_op jit(solution)/shard_map/all_to_all | solution.py:212
  212.4 12.2 %shard_map.85 = f32[2048,128]{1,0:T(8,128)S(1)} custom-call(bf16[2048,128]{1,0:T(8,128)(2,1)S(1)} %bitcast.107, bf16[2048,128]{1,0:T(8,128)(2,1)S(1)} %bitcast.103, s32[2048,128]{1,0:T(8,128)S(1)} %pad.24.name_ref), custom_call_target="tpu_custom_call" | custom-call | tf_op jit(solution)/shard_map/pallas_call | solution.py:64
  224.6 1.9 all_to_all.34
  226.5 3.7 all-to-all-start.2
  230.3 1.5 fusion.14
  232.1 0.8 gather_fusion
  232.9 4.7 all-to-all-done.2
  238.3 1.0 broadcast_in_dim.18
  239.3 2.6 all-to-all-start.3
  242.2 1.5 maximum_convert_fusion
  243.7 3.0 copy.114
  246.6 11.5 %all-to-all-done.3 = bf16[32,64,128]{2,1,0:T(8,128)(2,1)S(1)} async-done(((bf16[32,64,128]{2,1,0:T(8,128)(2,1)}), bf16[32,64,128]{2,1,0:T(8,128)(2,1)S(1)}, u32[]{:S(2)}, u32[]{:S(2)}) %all-to-all-start.3) | async-done | bytes 524320 | tf_op jit(solution)/shard_map/all_to_all | solution.py:243
  258.2 0.9 slice_add_fusion
  259.1 4.8 slice_reduce_fusion.7
  264.2 18.4 %shard_map.86 = (f32[2048,128]{1,0:T(8,128)S(1)}, f32[2048,128]{1,0:T(8,128)S(1)}, f32[1,2048]{1,0:T(1,128)S(1)}) custom-call(bf16[2048,128]{1,0:T(8,128)(2,1)S(1)} %bitcast.109, bf16[2048,128]{1,0:T(8,128)(2,1)S(1)} %bitcast.105, s32[2048,128]{1,0:T(8,128)S(1)} %pad.24.name_ref, f32[2048,128]{1,0:T(8,128)S(1)} %select_maximum_fusion.pack_ref, ...), custom_call_target="tpu_custom_call" | custom-call | tf_op jit(solution)/shard_map/pallas_call | solution.py:129
  282.8 2.7 maximum_multiply_fusion
  285.5 3.0 copy.115
  288.6 2.3 multiply_convert_fusion
  291.0 1.1 fusion.30
  292.9 8.6 %copy.113 = bf16[2,8,4,64,1024]{4,3,2,1,0:T(8,128)(2,1)} copy(bf16[2,8,4,64,1024]{4,3,0,1,2:T(8,128)(2,1)} %bitcast.119) | data formatting | bytes 16777216 | tf_op jit(solution)/shard_map/transpose | solution.py:195
  301.5 36.2 %all-gather.10.cloned.1.call-done = bf16[512,4112]{1,0:T(8,128)(2,1)} async-done(((bf16[64,4112]{1,0:T(8,128)(2,1)}), bf16[512,4112]{1,0:T(8,128)(2,1)}) %all-gather.10.cloned.1.call-update) | async-done | bytes 4210704 | tf_op jit(solution)/shard_map/all_gather | solution.py:277
  337.7 0.9 slice.174
  338.7 9.1 %fusion.5 = bf16[1024,512]{1,0:T(8,128)(2,1)S(1)} fusion(bf16[4096,1024]{1,0:T(8,128)(2,1)} %bitcast.120, bf16[512,4112]{1,0:T(8,128)(2,1)} %all-gather.10.cloned.1.call-done), kind=kOutput, calls=%fused_computation.18 | convolution fusion | flops 4295491584 | bytes 13631488 | tf_op jit(solution)/shard_map/dot_general | solution.py:278
  347.9 1.1 pad_maximum_fusion.1
  349.0 36.9 %all-gather.12.cloned.1.call-done = bf16[512,4112]{1,0:T(8,128)(2,1)} async-done(((bf16[64,4112]{1,0:T(8,128)(2,1)}), bf16[512,4112]{1,0:T(8,128)(2,1)}) %all-gather.12.cloned.1.call-update) | async-done | bytes 4210704 | tf_op jit(solution)/shard_map/all_gather | solution.py:277
  385.9 0.9 slice.177
  386.9 9.1 %fusion.8 = bf16[1024,512]{1,0:T(8,128)(2,1)S(1)} fusion(bf16[4096,1024]{1,0:T(8,128)(2,1)} %bitcast.121, bf16[512,4112]{1,0:T(8,128)(2,1)} %all-gather.12.cloned.1.call-done), kind=kOutput, calls=%fused_computation.19 | convolution fusion | flops 4295491584 | bytes 13631488 | tf_op jit(solution)/shard_map/dot_general | solution.py:278
  396.1 1.0 pad_maximum_fusion.2
  397.8 41.9 %all-gather.14.cloned.1.call-done = bf16[4160,512]{1,0:T(8,128)(2,1)} async-done(((bf16[1040,512]{1,0:T(8,128)(2,1)}), bf16[4160,512]{1,0:T(8,128)(2,1)}) %all-gather.14.cloned.1.call-update) | async-done | bytes 4259856 | tf_op jit(solution)/shard_map/all_gather | solution.py:285
  439.7 0.8 slice_bitcast_fusion.1
  440.5 54.8 %all-gather.16.cloned.1.call-done = bf16[4160,512]{1,0:T(8,128)(2,1)} async-done(((bf16[1040,512]{1,0:T(8,128)(2,1)}), bf16[4160,512]{1,0:T(8,128)(2,1)}) %all-gather.16.cloned.1.call-update) | async-done | bytes 4259856 | tf_op jit(solution)/shard_map/all_gather | solution.py:285
  495.2 0.8 slice_bitcast_fusion
  496.0 2.2 copy-done
  498.2 2.2 copy-done.1
  500.4 8.6 %shard_map.87 = f32[1024,4096]{1,0:T(8,128)} custom-call(bf16[4,1040,512]{2,1,0:T(8,128)(2,1)S(1)} %bitcast.112, bf16[4,1040,512]{2,1,0:T(8,128)(2,1)S(1)} %bitcast.114), custom_call_target="tpu_custom_call" | custom-call | tf_op jit(solution)/shard_map/pallas_call | solution.py:164
  (89 shorter events, 6.8 us)
Async XLA Ops:
  8.0 146.2 %all-gather.8.cloned.1.call-start = ((), (), s32[]{:S(2)}) async-start(), calls=%async_computation.6 | async-start | bytes 10485760 | tf_op jit(solution)/shard_map/all_gather | solution.py:191
  67.5 1.6 copy-start.5
  67.5 104.3 %reduce-scatter.2.cloned.1.call-start = ((), (), s32[]{:S(2)}) async-start(), calls=%async_computation.5 | async-start | bytes 9437184 | tf_op jit(solution)/shard_map/reduce_scatter | solution.py:188
  83.3 0.7 copy-start.8
  83.3 0.7 copy-start.9
  83.3 88.5 %copy-start.2 = (bf16[2,64,4096]{2,1,0:T(8,128)(2,1)S(1)}, bf16[2,64,4096]{2,1,0:T(8,128)(2,1)}, u32[]{:S(2)}) copy-start(bf16[2,64,4096]{2,1,0:T(8,128)(2,1)} %param.7) | copy-start | bytes 3145732
  84.0 89.5 %copy-start.7 = (f32[4096]{0:T(1024)S(1)}, f32[4096]{0:T(1024)}, u32[]{:S(2)}) copy-start(f32[4096]{0:T(1024)} %param.9) | copy-start | bytes 49156
  171.8 1.8 copy-start.3
  174.9 1.1 copy-start.6
  179.4 32.2 %all-to-all-start.1 = ((bf16[32,144,128]{2,1,0:T(8,128)(2,1)}), bf16[32,144,128]{2,1,0:T(8,128)(2,1)S(1)}, u32[]{:S(2)}, u32[]{:S(2)}) async-start(bf16[32,144,128]{2,1,0:T(8,128)(2,1)} %copy.107), calls=%async_computation.2 | async-start | bytes 2359296 | tf_op jit(solution)/shard_map/all_to_all | solution.py:212
  226.5 11.1 %all-to-all-start.2 = ((f32[32,1,448]{2,1,0:T(1,128)}), f32[32,1,448]{2,1,0:T(1,128)S(1)}, u32[]{:S(2)}, u32[]{:S(2)}) async-start(f32[32,1,448]{2,1,0:T(1,128)} %all_to_all.34), calls=%async_computation.3 | async-start | bytes 131072 | tf_op jit(solution)/shard_map/all_to_all | solution.py:222
  239.3 18.9 %all-to-all-start.3 = ((bf16[32,64,128]{2,1,0:T(8,128)(2,1)}), bf16[32,64,128]{2,1,0:T(8,128)(2,1)S(1)}, u32[]{:S(2)}, u32[]{:S(2)}) async-start(bf16[32,64,128]{2,1,0:T(8,128)(2,1)} %broadcast_in_dim.18), calls=%async_computation.4 | async-start | bytes 1048576 | tf_op jit(solution)/shard_map/all_to_all | solution.py:243
  241.9 95.9 %all-gather.10.cloned.1.call-start = ((), (), s32[]{:S(2)}) async-start(), calls=%async_computation.7 | async-start | bytes 4866048 | tf_op jit(solution)/shard_map/all_gather | solution.py:277
  285.4 3.2 copy-start.4
  292.1 93.8 %all-gather.12.cloned.1.call-start = ((), (), s32[]{:S(2)}) async-start(), calls=%async_computation.8 | async-start | bytes 4866048 | tf_op jit(solution)/shard_map/all_gather | solution.py:277
  292.7 147.0 %all-gather.14.cloned.1.call-start = ((), (), s32[]{:S(2)}) async-start(), calls=%async_computation.9 | async-start | bytes 5324800 | tf_op jit(solution)/shard_map/all_gather | solution.py:285
  349.0 146.2 %all-gather.16.cloned.1.call-start = ((), (), s32[]{:S(2)}) async-start(), calls=%async_computation.10 | async-start | bytes 5324800 | tf_op jit(solution)/shard_map/all_gather | solution.py:285
  496.0 2.2 copy-start
  498.2 2.2 copy-start.1
Sparse Core Ops, SparseCore 0:
  67.6 86.5 all-gather.7
Sparse Core Ops, SparseCore 1:
  83.4 88.3 reduce-scatter.1
  292.2 45.5 all-gather.9
  339.3 46.6 all-gather.11
  387.8 51.8 all-gather.13
  442.1 53.1 all-gather.15

commit v4 on v3

--- a/solution.py
+++ b/solution.py
@@ -150,25 +150,46 @@
     )(queries, passages, names, pack, widen)
 
 
-def lay_kernel(*refs):
+def lay_kernel(count, me_ref, *refs):
     *pieces, out_ref = refs
-    span = pieces[0].shape[2]
-    for at, piece in enumerate(pieces):
-        out_ref[:, at * span : (at + 1) * span] = piece[0].astype(jnp.float32)
-
-
-def lay_columns(pieces, hidden):
-    parts, _, span = pieces[0].shape
-    block = min(hidden, 256)
-    wide = span * len(pieces)
+    span = pieces[0].shape[1]
+    wide = span * PIECES
+    for piece in range(PIECES):
+        for turn in range(count):
+            at = (me_ref[0] ^ turn) * wide + piece * span
+            here = pieces[piece * count + turn][...].astype(jnp.float32)
+            out_ref[:, pl.ds(pl.multiple_of(at, span), span)] = here
+
+
+def lay_columns(me, pieces, hidden):
+    count, span = len(pieces[0]), pieces[0][0].shape[1]
+    block = min(hidden, 128)
+    width = count * PIECES * span
     return pl.pallas_call(
-        lay_kernel,
-        grid=(parts, hidden // block),
-        in_specs=[pl.BlockSpec((1, block, span), lambda r, i: (r, i, 0)) for _ in pieces],
-        out_specs=pl.BlockSpec((block, wide), lambda r, i: (i, r)),
-        out_shape=jax.ShapeDtypeStruct((hidden, parts * wide), jnp.float32),
+        functools.partial(lay_kernel, count),
+        grid_spec=pltpu.PrefetchScalarGridSpec(
+            num_scalar_prefetch=1,
+            grid=(hidden // block,),
+            in_specs=[pl.BlockSpec((block, span), lambda i, m: (i, 0))] * (PIECES * count),
+            out_specs=pl.BlockSpec((block, width), lambda i, m: (i, 0)),
+        ),
+        out_shape=jax.ShapeDtypeStruct((hidden, width), jnp.float32),
         compiler_params=pltpu.CompilerParams(vmem_limit_bytes=32 * 1024 * 1024),
-    )(*pieces)
+    )(me.reshape(1), *[block for piece in pieces for block in piece])
+
+
+def exchange(mine):
+    count = lax.axis_size("replica")
+
+    def swap(block, turn):
+        return lax.ppermute(block, "replica", [(i, i ^ turn) for i in range(count)])
+
+    if count != 4:
+        return [mine] + [swap(mine, turn) for turn in range(1, count)]
+    first, second = swap(mine, 1), swap(mine, 2)
+    half = mine.shape[0] // 32 * 16
+    across = [swap(first[:half], 2), swap(second[half:], 1)]
+    return [mine, first, second, jnp.concatenate(across, axis=0)]
 
 
 def per_device(activations, residual, down_weight, norm_gain, hard_owner, hard_row):
@@ -282,10 +303,17 @@
             preferred_element_type=jnp.float32,
         ).astype(jnp.bfloat16)
         product = jnp.concatenate([product, columns[:, 2 * total :].T], axis=0)
-        pieces.append(lax.all_gather(product, "replica", axis=0, tiled=False))
-    weight_grad = lay_columns(pieces, hidden)
-    gain_grad = jnp.stack([piece[:, hidden : hidden + 3] for piece in pieces], axis=1)
-    gain_grad = jnp.sum(gain_grad.astype(jnp.float32), axis=2).reshape(width)
+        pieces.append(exchange(product))
+    me = lax.axis_index("replica")
+    weight_grad = lay_columns(me, pieces, hidden)
+    gain_grad = jnp.stack(
+        [
+            jnp.stack([jnp.sum(b[hidden : hidden + 3].astype(jnp.float32), axis=0) for b in blocks])
+            for blocks in pieces
+        ],
+        axis=1,
+    )
+    gain_grad = gain_grad[jnp.arange(n_replica) ^ me].reshape(width)
     return (mean_loss, weight_grad, gain_grad)
 
 

time: 519 us -> 470 us (0.906)
  waiting for transfers between devices: 303 us -> 239 us
  starting transfers between devices: 9.89 us -> 20 us
    all_gather x2 -> x0, waiting for transfers between devices: 96.7 us -> none  [per_device(): pieces.append(lax.all_gather(product, 'replica', axis=0, tiled=False))]
    ppermute x0 -> x8, waiting for transfers between devices: none -> 34.3 us  [swap(): return lax.ppermute(block, 'replica', [(i, i ^ turn) for i in range(count)])]
    ppermute x0 -> x8, starting transfers between devices: none -> 10.2 us  [swap(): return lax.ppermute(block, 'replica', [(i, i ^ turn) for i in range(count)])]
    unnamed x31 -> x33, local copies, waits for them, and re-layouts: 11 us -> 8.16 us
  transfers between devices with their start and end apart: 9 -> 15, of which waited for: 9 -> 10; matrix products, arithmetic and copies ran while one was open for 10% -> 13% of each run, Pallas kernels for 0% -> 0%
where the time goes in v4:
time: 470 us; the launch traced here: 468 us
  waiting for transfers between devices  239 us (51%)
  blocking collectives  55.3 us (12%)
  local copies, waits for them, and re-layouts  41.2 us (9%)
  Pallas kernels  39.5 us (8%)
  matrix products  33.9 us (7%)
  other arithmetic  21.6 us (5%)
  starting transfers between devices  20 us (4%)
  between operations  17.9 us (4%)
    all_gather x2, waiting for transfers between devices, per_device(): columns = lax.all_gather(mine, 'shard', axis=0, tiled=True)  71.5 us
    all_gather x1, waiting for transfers between devices, per_device(): all_rows = lax.all_gather(spread_rows, 'replica', axis=0, tiled=False)  70 us
    all_to_all x1, blocking collectives, per_device(): lax.all_to_all(rows, 'shard', split_axis=1, concat_axis=0, tiled=True)  55.3 us
    ppermute x8, waiting for transfers between devices, swap(): return lax.ppermute(block, 'replica', [(i, i ^ turn) for i in range(count)])  34.3 us
    all_to_all x1, waiting for transfers between devices, per_device(): lax.all_to_all(cut, everywhere, split_axis=0, concat_axis=0, tiled=True)  29.1 us
    pallas_call x1, Pallas kernels, spread_grads(): pl.pallas_call(functools.partial(spread_kernel, group_rows), grid=(total...  18.4 us
    dot_general x2, matrix products, per_device(): lax.dot_general(all_rows, columns[:, :2 * total], (((0,), (1,)), ((), ())...  18.2 us
    reduce_scatter x1, waiting for transfers between devices, per_device(): lax.psum_scatter(terms.astype(jnp.bfloat16), 'shard', scatter_dimension=0...  17.6 us
  transfers between devices with their start and end apart: 15, of which 10 were waited for; matrix products, arithmetic and copies ran while one was open for 13% of the time, Pallas kernels for 0%

profile of v4, /device:TPU:0, one launch (start us, length us, event | category | flops | bytes accessed | tf_op | source)
XLA Modules:
  0.0 468.3 jit_solution(1172089371311867012)
XLA Ops:
  8.0 3.0 copy.122
  11.0 1.2 copy.101
  12.2 55.3 %all_to_all.39 = bf16[128,8,1024]{2,0,1:T(8,128)(2,1)} all-to-all(bf16[128,8,1024]{2,0,1:T(8,128)(2,1)S(1)} %copy.101), channel_id=1, replica_groups=mesh['shard'=8,'replica'=4] {'shard'}, dimensions={1} | all-to-all | bytes 4194304 | tf_op jit(solution)/shard_map/all_to_all | solution.py:207
  67.6 1.5 copy-done.3
  69.1 14.2 %convolution_convert_fusion = bf16[1024,4096]{1,0:T(8,128)(2,1)} fusion(bf16[1024,1024]{1,0:T(8,128)(2,1)S(1)} %bitcast.122, bf16[1024,4096]{1,0:T(8,128)(2,1)} %param.8), kind=kOutput, calls=%fused_computation.2 | convolution fusion | flops 8594128896 | bytes 18874368 | tf_op jit(solution)/shard_map/dot_general | solution.py:208
  84.2 70.0 %all-gather.4.cloned.1.call-done = bf16[4,1024,1024]{2,1,0:T(8,128)(2,1)} async-done(((bf16[1,1024,1024]{2,1,0:T(8,128)(2,1)}), bf16[4,1024,1024]{2,1,0:T(8,128)(2,1)}) %all-gather.4.cloned.1.call-update) | async-done | bytes 8388624 | tf_op jit(solution)/shard_map/all_gather | solution.py:212
  154.2 17.6 %reduce-scatter.2.cloned.1.call-done = bf16[128,4096]{1,0:T(8,128)(2,1)} async-done(((bf16[1024,4096]{1,0:T(8,128)(2,1)}), bf16[128,4096]{1,0:T(8,128)(2,1)}) %reduce-scatter.2.cloned.1.call-update) | async-done | bytes 1048592 | tf_op jit(solution)/shard_map/reduce_scatter | solution.py:209
  171.8 1.7 multiply_reduce_fusion.3
  176.8 2.7 copy.105
  179.4 3.1 all-to-all-start.1
  182.5 29.1 %all-to-all-done.1 = bf16[32,144,128]{2,1,0:T(8,128)(2,1)S(1)} async-done(((bf16[32,144,128]{2,1,0:T(8,128)(2,1)}), bf16[32,144,128]{2,1,0:T(8,128)(2,1)S(1)}, u32[]{:S(2)}, u32[]{:S(2)}) %all-to-all-start.1) | async-done | bytes 1179680 | tf_op jit(solution)/shard_map/all_to_all | solution.py:233
  212.4 12.2 %shard_map.85 = f32[2048,128]{1,0:T(8,128)S(1)} custom-call(bf16[2048,128]{1,0:T(8,128)(2,1)S(1)} %bitcast.110, bf16[2048,128]{1,0:T(8,128)(2,1)S(1)} %bitcast.106, s32[2048,128]{1,0:T(8,128)S(1)} %pad.24.name_ref), custom_call_target="tpu_custom_call" | custom-call | tf_op jit(solution)/shard_map/pallas_call | solution.py:64
  224.6 1.9 all_to_all.34
  226.5 3.7 all-to-all-start.2
  230.3 1.5 fusion.14
  232.9 4.7 %all-to-all-done.2 = f32[32,1,448]{2,1,0:T(1,128)S(1)} async-done(((f32[32,1,448]{2,1,0:T(1,128)}), f32[32,1,448]{2,1,0:T(1,128)S(1)}, u32[]{:S(2)}, u32[]{:S(2)}) %all-to-all-start.2) | async-done | bytes 57376 | tf_op jit(solution)/shard_map/all_to_all | solution.py:243
  238.3 1.0 broadcast_in_dim.18
  239.3 2.6 all-to-all-start.3
  242.2 1.5 maximum_convert_fusion
  243.7 3.0 copy.112
  246.6 11.5 %all-to-all-done.3 = bf16[32,64,128]{2,1,0:T(8,128)(2,1)S(1)} async-done(((bf16[32,64,128]{2,1,0:T(8,128)(2,1)}), bf16[32,64,128]{2,1,0:T(8,128)(2,1)S(1)}, u32[]{:S(2)}, u32[]{:S(2)}) %all-to-all-start.3) | async-done | bytes 524320 | tf_op jit(solution)/shard_map/all_to_all | solution.py:264
  259.1 4.8 %slice_reduce_fusion.7 = (f32[2048]{0:T(1024)S(1)}, f32[2048]{0:T(1024)S(1)}, f32[2048]{0:T(1024)S(1)}, f32[2048]{0:T(1024)S(1)}, f32[2048]{0:T(1024)S(1)}, /*in...) fusion(f32[2048,16]{1,0:T(8,128)S(1)} %slice_add_fusion), kind=kLoop, calls=%fused_computation.36 | loop fusion | flops 2047 | bytes 139268 | tf_op jit(solution)/shard_map/slice | solution.py:273
  264.2 18.4 %shard_map.86 = (f32[2048,128]{1,0:T(8,128)S(1)}, f32[2048,128]{1,0:T(8,128)S(1)}, f32[1,2048]{1,0:T(1,128)S(1)}) custom-call(bf16[2048,128]{1,0:T(8,128)(2,1)S(1)} %bitcast.112, bf16[2048,128]{1,0:T(8,128)(2,1)S(1)} %bitcast.108, s32[2048,128]{1,0:T(8,128)S(1)} %pad.24.name_ref, f32[2048,128]{1,0:T(8,128)S(1)} %select_maximum_fusion.pack_ref, ...), custom_call_target="tpu_custom_call" | custom-call | tf_op jit(solution)/shard_map/pallas_call | solution.py:129
  282.8 2.7 maximum_multiply_fusion
  285.5 3.0 copy.113
  288.6 2.3 multiply_convert_fusion
  291.0 1.1 fusion.31
  292.7 8.6 %copy.111 = bf16[2,8,4,64,1024]{4,3,2,1,0:T(8,128)(2,1)} copy(bf16[2,8,4,64,1024]{4,3,0,1,2:T(8,128)(2,1)} %bitcast.118) | data formatting | bytes 16777216 | tf_op jit(solution)/shard_map/transpose | solution.py:216
  301.3 36.5 %all-gather.6.cloned.1.call-done = bf16[512,4112]{1,0:T(8,128)(2,1)} async-done(((bf16[64,4112]{1,0:T(8,128)(2,1)}), bf16[512,4112]{1,0:T(8,128)(2,1)}) %all-gather.6.cloned.1.call-update) | async-done | bytes 4210704 | tf_op jit(solution)/shard_map/all_gather | solution.py:298
  337.7 0.9 slice.216
  338.7 9.1 %fusion.5 = bf16[1024,512]{1,0:T(8,128)(2,1)S(1)} fusion(bf16[4096,1024]{1,0:T(8,128)(2,1)} %bitcast.119, bf16[512,4112]{1,0:T(8,128)(2,1)} %all-gather.6.cloned.1.call-done), kind=kOutput, calls=%fused_computation.19 | convolution fusion | flops 4295491584 | bytes 13631488 | tf_op jit(solution)/shard_map/dot_general | solution.py:299
  347.9 1.5 collective-permute-start.1
  349.5 1.5 collective-permute-start
  350.9 35.0 %all-gather.8.cloned.1.call-done = bf16[512,4112]{1,0:T(8,128)(2,1)} async-done(((bf16[64,4112]{1,0:T(8,128)(2,1)}), bf16[512,4112]{1,0:T(8,128)(2,1)}) %all-gather.8.cloned.1.call-update) | async-done | bytes 4210704 | tf_op jit(solution)/shard_map/all_gather | solution.py:298
  386.9 9.1 %fusion.8 = bf16[1024,512]{1,0:T(8,128)(2,1)S(1)} fusion(bf16[4096,1024]{1,0:T(8,128)(2,1)} %bitcast.120, bf16[512,4112]{1,0:T(8,128)(2,1)} %all-gather.8.cloned.1.call-done), kind=kOutput, calls=%fused_computation.20 | convolution fusion | flops 4295491584 | bytes 13631488 | tf_op jit(solution)/shard_map/dot_general | solution.py:299
  396.1 1.5 collective-permute-start.5
  397.7 1.5 collective-permute-start.4
  400.5 1.9 slice.217
  403.0 19.7 %collective-permute-done.5.refs_6_ = bf16[1040,512]{1,0:T(8,128)(2,1)} collective-permute-done((bf16[1040,512]{1,0:T(8,128)(2,1)S(1)}, bf16[1040,512]{1,0:T(8,128)(2,1)}, u32[]{:S(2)}, u32[]{:S(2)}) %collective-permute-start.5) | collective-permute-done | bytes 1064992 | tf_op jit(solution)/shard_map/ppermute | solution.py:185
  422.6 1.1 slice.223
  423.7 1.5 collective-permute-start.7
  425.3 1.9 slice.222
  427.2 1.5 collective-permute-start.6
  430.8 4.8 %collective-permute-done.3 = bf16[528,512]{1,0:T(8,128)(2,1)S(1)} collective-permute-done((bf16[528,512]{1,0:T(8,128)(2,1)S(1)}, bf16[528,512]{1,0:T(8,128)(2,1)S(1)}, u32[]{:S(2)}, u32[]{:S(2)}) %collective-permute-start.3) | collective-permute-done | bytes 540704 | tf_op jit(solution)/shard_map/ppermute | solution.py:185
  436.5 9.8 %collective-permute-done.7 = bf16[528,512]{1,0:T(8,128)(2,1)S(1)} collective-permute-done((bf16[528,512]{1,0:T(8,128)(2,1)S(1)}, bf16[528,512]{1,0:T(8,128)(2,1)S(1)}, u32[]{:S(2)}, u32[]{:S(2)}) %collective-permute-start.7) | collective-permute-done | bytes 540704 | tf_op jit(solution)/shard_map/ppermute | solution.py:185
  448.3 1.3 pad_maximum_fusion.2.refs_3_
  449.6 1.1 pad_maximum_fusion.4.refs_7_
  450.7 8.9 %shard_map.87 = f32[1024,4096]{1,0:T(8,128)} custom-call(s32[1]{0:T(128)} %bitcast.24.me_ref, bf16[1040,512]{1,0:T(8,128)(2,1)S(1)} %pad_maximum_fusion.1.refs_0_, bf16[1040,512]{1,0:T(8,128)(2,1)} %collective-permute-done.refs_1_, bf16[1040,512]{1,0:T(8,128)(2,1)S(1)} %collective-permute-done.1.refs_2_, bf16[1040,512]{1,0:T(8,128)(2,1)S(1)} %pad_maximum_fusion.2.refs_3_, ...), custom_call_target="tpu_custom_call" | custom-call | tf_op jit(solution)/shard_map/pallas_call | solution.py:168
  (119 shorter events, 16.9 us)
Async XLA Ops:
  8.0 146.2 %all-gather.4.cloned.1.call-start = ((), (), s32[]{:S(2)}) async-start(), calls=%async_computation.6 | async-start | bytes 10485760 | tf_op jit(solution)/shard_map/all_gather | solution.py:212
  67.5 1.6 copy-start.3
  67.5 104.3 %reduce-scatter.2.cloned.1.call-start = ((), (), s32[]{:S(2)}) async-start(), calls=%async_computation.5 | async-start | bytes 9437184 | tf_op jit(solution)/shard_map/reduce_scatter | solution.py:209
  83.3 0.7 copy-start.9
  83.3 0.7 copy-start.10
  83.3 88.5 %copy-start = (bf16[2,64,4096]{2,1,0:T(8,128)(2,1)S(1)}, bf16[2,64,4096]{2,1,0:T(8,128)(2,1)}, u32[]{:S(2)}) copy-start(bf16[2,64,4096]{2,1,0:T(8,128)(2,1)} %param.7) | copy-start | bytes 3145732
  84.0 89.5 %copy-start.8 = (f32[4096]{0:T(1024)S(1)}, f32[4096]{0:T(1024)}, u32[]{:S(2)}) copy-start(f32[4096]{0:T(1024)} %param.9) | copy-start | bytes 49156
  171.8 1.8 copy-start.1
  174.9 1.1 copy-start.4
  179.4 32.2 %all-to-all-start.1 = ((bf16[32,144,128]{2,1,0:T(8,128)(2,1)}), bf16[32,144,128]{2,1,0:T(8,128)(2,1)S(1)}, u32[]{:S(2)}, u32[]{:S(2)}) async-start(bf16[32,144,128]{2,1,0:T(8,128)(2,1)} %copy.105), calls=%async_computation.2 | async-start | bytes 2359296 | tf_op jit(solution)/shard_map/all_to_all | solution.py:233
  226.5 11.1 %all-to-all-start.2 = ((f32[32,1,448]{2,1,0:T(1,128)}), f32[32,1,448]{2,1,0:T(1,128)S(1)}, u32[]{:S(2)}, u32[]{:S(2)}) async-start(f32[32,1,448]{2,1,0:T(1,128)} %all_to_all.34), calls=%async_computation.3 | async-start | bytes 131072 | tf_op jit(solution)/shard_map/all_to_all | solution.py:243
  239.3 18.9 %all-to-all-start.3 = ((bf16[32,64,128]{2,1,0:T(8,128)(2,1)}), bf16[32,64,128]{2,1,0:T(8,128)(2,1)S(1)}, u32[]{:S(2)}, u32[]{:S(2)}) async-start(bf16[32,64,128]{2,1,0:T(8,128)(2,1)} %broadcast_in_dim.18), calls=%async_computation.4 | async-start | bytes 1048576 | tf_op jit(solution)/shard_map/all_to_all | solution.py:264
  241.9 95.9 %all-gather.6.cloned.1.call-start = ((), (), s32[]{:S(2)}) async-start(), calls=%async_computation.7 | async-start | bytes 4866048 | tf_op jit(solution)/shard_map/all_gather | solution.py:298
  285.4 3.2 copy-start.2
  292.1 93.8 %all-gather.8.cloned.1.call-start = ((), (), s32[]{:S(2)}) async-start(), calls=%async_computation.8 | async-start | bytes 4866048 | tf_op jit(solution)/shard_map/all_gather | solution.py:298
  347.9 51.9 %collective-permute-start.1 = (bf16[1040,512]{1,0:T(8,128)(2,1)S(1)}, bf16[1040,512]{1,0:T(8,128)(2,1)S(1)}, u32[]{:S(2)}, u32[]{:S(2)}) collective-permute-start(bf16[1040,512]{1,0:T(8,128)(2,1)S(1)} %pad_maximum_fusion.1.refs_0_), channel_id=1, source_target_pairs={{0,2},{1,3},{2,0},{3,1},{4,6},{5,7},{6,4},{7,5},{8,10},{9,11},{10,... | collective-permute-start | bytes 3194888 | tf_op jit(solution)/shard_map/ppermute | solution.py:185
  349.5 51.0 %collective-permute-start = (bf16[1040,512]{1,0:T(8,128)(2,1)S(1)}, bf16[1040,512]{1,0:T(8,128)(2,1)}, u32[]{:S(2)}, u32[]{:S(2)}) collective-permute-start(bf16[1040,512]{1,0:T(8,128)(2,1)S(1)} %pad_maximum_fusion.1.refs_0_), channel_id=1, source_target_pairs={{0,1},{1,0},{2,3},{3,2},{4,5},{5,4},{6,7},{7,6},{8,9},{9,8},{10,11... | collective-permute-start | bytes 3194888 | tf_op jit(solution)/shard_map/ppermute | solution.py:185
  396.1 26.5 %collective-permute-start.5 = (bf16[1040,512]{1,0:T(8,128)(2,1)S(1)}, bf16[1040,512]{1,0:T(8,128)(2,1)}, u32[]{:S(2)}, u32[]{:S(2)}) collective-permute-start(bf16[1040,512]{1,0:T(8,128)(2,1)S(1)} %pad_maximum_fusion.3.refs_4_), channel_id=1, source_target_pairs={{0,2},{1,3},{2,0},{3,1},{4,6},{5,7},{6,4},{7,5},{8,10},{9,11},{10,... | collective-permute-start | bytes 3194888 | tf_op jit(solution)/shard_map/ppermute | solution.py:185
  397.7 27.6 %collective-permute-start.4 = (bf16[1040,512]{1,0:T(8,128)(2,1)S(1)}, bf16[1040,512]{1,0:T(8,128)(2,1)}, u32[]{:S(2)}, u32[]{:S(2)}) collective-permute-start(bf16[1040,512]{1,0:T(8,128)(2,1)S(1)} %pad_maximum_fusion.3.refs_4_), channel_id=1, source_target_pairs={{0,1},{1,0},{2,3},{3,2},{4,5},{5,4},{6,7},{7,6},{8,9},{9,8},{10,11... | collective-permute-start | bytes 3194888 | tf_op jit(solution)/shard_map/ppermute | solution.py:185
  399.9 35.8 %collective-permute-start.3 = (bf16[528,512]{1,0:T(8,128)(2,1)S(1)}, bf16[528,512]{1,0:T(8,128)(2,1)S(1)}, u32[]{:S(2)}, u32[]{:S(2)}) collective-permute-start(bf16[528,512]{1,0:T(8,128)(2,1)S(1)} %slice.218), channel_id=1, source_target_pairs={{0,1},{1,0},{2,3},{3,2},{4,5},{5,4},{6,7},{7,6},{8,9},{9,8},{10,11... | collective-permute-start | bytes 1622024 | tf_op jit(solution)/shard_map/ppermute | solution.py:185
  402.4 45.9 %collective-permute-start.2 = (bf16[512,512]{1,0:T(8,128)(2,1)}, bf16[512,512]{1,0:T(8,128)(2,1)}, u32[]{:S(2)}, u32[]{:S(2)}) collective-permute-start(bf16[512,512]{1,0:T(8,128)(2,1)} %slice.217), channel_id=1, source_target_pairs={{0,2},{1,3},{2,0},{3,1},{4,6},{5,7},{6,4},{7,5},{8,10},{9,11},{10,... | collective-permute-start | bytes 1572872 | tf_op jit(solution)/shard_map/ppermute | solution.py:185
  423.7 22.5 %collective-permute-start.7 = (bf16[528,512]{1,0:T(8,128)(2,1)S(1)}, bf16[528,512]{1,0:T(8,128)(2,1)S(1)}, u32[]{:S(2)}, u32[]{:S(2)}) collective-permute-start(bf16[528,512]{1,0:T(8,128)(2,1)S(1)} %slice.223), channel_id=1, source_target_pairs={{0,1},{1,0},{2,3},{3,2},{4,5},{5,4},{6,7},{7,6},{8,9},{9,8},{10,11... | collective-permute-start | bytes 1622024 | tf_op jit(solution)/shard_map/ppermute | solution.py:185
  427.2 22.4 %collective-permute-start.6 = (bf16[512,512]{1,0:T(8,128)(2,1)}, bf16[512,512]{1,0:T(8,128)(2,1)}, u32[]{:S(2)}, u32[]{:S(2)}) collective-permute-start(bf16[512,512]{1,0:T(8,128)(2,1)} %slice.222), channel_id=1, source_target_pairs={{0,2},{1,3},{2,0},{3,1},{4,6},{5,7},{6,4},{7,5},{8,10},{9,11},{10,... | collective-permute-start | bytes 1572872 | tf_op jit(solution)/shard_map/ppermute | solution.py:185
  435.6 0.8 copy-start.5
  446.2 0.8 copy-start.6
  447.7 1.9 copy-start.7
Sparse Core Ops, SparseCore 0:
  67.6 86.5 all-gather.3
Sparse Core Ops, SparseCore 1:
  83.4 88.3 reduce-scatter.1
  292.2 45.5 all-gather.5
  339.3 46.6 all-gather.7
